TPU v7x, 256 devices: a whole 4x4x8 slice. The times are simulated.
256 devices in a mesh: probe: 64 (over x, z, y_lo), slab: 4 (over y_hi, core).
Axes of the slice: x: 4, y: 4 (y_hi: 2, y_lo: 2; y = y_hi * 2 + y_lo), z: 8, core: 2. Of those that a mesh axis runs over, the one named last changes fastest.
Arguments:
- incident_prev: float32 [128, 256, 512], P('slab', 'probe'), may hold values from -6 to 6
- incident_now: float32 [128, 256, 512], P('slab', 'probe'), may hold values from -6 to 6
- forcing: float32 [2, 128, 256, 512], P(None, 'slab', 'probe'), may hold values from -4 to 4
- stiffness: float32 [128, 256, 512], P('slab', 'probe'), may hold values from 0.05 to 0.2
- probe_prev: float32 [128, 2048, 512], P('slab', 'probe'), may hold values from -6 to 6
- probe_now: float32 [128, 2048, 512], P('slab', 'probe'), may hold values from -6 to 6
- perturb: float32 [128, 2048, 512], P('slab', 'probe'), may hold values from -4 to 4
Outputs:
- probe_out: float32 [128, 2048, 512], P('slab', 'probe')
- incident_out: float32 [128, 256, 512], P('slab', 'probe')
All inputs are finite; a program needn't handle non-finite values.
Results may differ from a plain program's by a relative error of at most 0.00002.
Values sent between devices are 32-bit elements; how exact they have to be, the bound alone decides.
A program may use at most 128 MiB of HBM per device.

v0:
```python
import jax
import jax.numpy as jnp
from jax import lax
from jax.sharding import PartitionSpec as P

PROBES_ALL = 8
STEPS = 2


stencil_reach = 4
coefficients = (-205.0 / 72.0, 8.0 / 5.0, -1.0 / 5.0, 8.0 / 315.0, -1.0 / 560.0)


def partner_2(block, axis, bit):
    count = lax.axis_size(axis)
    route = []
    for low in range(count):
        high = low | 1 << bit
        if high != low and high < count:
            route += [(low, high), (high, low)]
    return lax.ppermute(block, axis, route)


def with_halo(block, sides, width):
    for axis, dim in sides:
        count = lax.axis_size(axis)
        forward = [(i, i + 1) for i in range(count - 1)]
        backward = [(target, source) for source, target in forward]
        low = lax.ppermute(
            lax.slice_in_dim(block, block.shape[dim] - width, None, axis=dim), axis, forward
        )
        high = lax.ppermute(lax.slice_in_dim(block, 0, width, axis=dim), axis, backward)
        block = jnp.concatenate([low, block, high], axis=dim)
    return block


def passed_along(value, axis, steps):
    count = lax.axis_size(axis)
    first, last = (max(0, -steps), min(count, count - steps))
    return lax.ppermute(value, axis, [(source, source + steps) for source in range(first, last)])


def laplace(extended, dims):
    middle = [slice(stencil_reach, size - stencil_reach) for d, size in enumerate(extended.shape)]
    summed = coefficients[0] * len(dims) * extended[tuple(middle)]
    for d in dims:
        n = extended.shape[d] - 2 * stencil_reach
        for j in range(1, 5):
            lower_cut = list(middle)
            lower_cut[d] = slice(stencil_reach - j, stencil_reach - j + n)
            upper_cut = list(middle)
            upper_cut[d] = slice(stencil_reach + j, stencil_reach + j + n)
            summed = summed + coefficients[j] * (
                extended[tuple(lower_cut)] + extended[tuple(upper_cut)]
            )
    return summed


def group_rows(block_rows):
    position = lax.axis_index("probe")
    for bit_index in range(PROBES_ALL.bit_length() - 1):
        partner = partner_2(block_rows, "probe", bit_index)
        leading = (position >> bit_index) % 2 == 0
        block_rows = jnp.where(
            leading,
            jnp.concatenate([block_rows, partner], 1),
            jnp.concatenate([partner, block_rows], 1),
        )
    return block_rows


def local(incident_prev, incident_now, forcing, stiffness, probe_prev, probe_now, perturb):
    laplacians = []
    block_stiff = group_rows(stiffness)
    previous, current = (incident_prev, incident_now)
    for moment in range(STEPS):
        extended = with_halo(current, (("probe", 1), ("slab", 0)), 4)
        extended = jnp.pad(extended, ((0, 0), (0, 0), (stencil_reach, stencil_reach)))
        laplacian = laplace(extended, (0, 1, 2))
        laplacians.append(group_rows(laplacian))
        previous, current = (
            current,
            2.0 * current - previous + stiffness * laplacian + forcing[moment],
        )
    older_field, newer_field = (probe_prev, probe_now)
    for moment in range(STEPS):
        lower_rim = passed_along(newer_field[:, -stencil_reach:], "probe", PROBES_ALL)
        upper_rim = passed_along(newer_field[:, :stencil_reach], "probe", -PROBES_ALL)
        rowed = jnp.concatenate([lower_rim, newer_field, upper_rim], 1)
        extended = with_halo(rowed, (("slab", 0),), 4)
        extended = jnp.pad(extended, ((0, 0), (0, 0), (stencil_reach, stencil_reach)))
        probe_lap = laplace(extended, (0, 1, 2))
        older_field, newer_field = (
            newer_field,
            2.0 * newer_field
            - older_field
            + block_stiff * probe_lap
            + 2.0 * block_stiff * perturb * laplacians[moment],
        )
    return (newer_field, current)


def solution(mesh):
    return jax.shard_map(
        local,
        mesh=mesh,
        in_specs=(
            P("slab", "probe", None),
            P("slab", "probe", None),
            P(None, "slab", "probe", None),
            P("slab", "probe", None),
            P("slab", "probe", None),
            P("slab", "probe", None),
            P("slab", "probe", None),
        ),
        out_specs=(P("slab", "probe", None), P("slab", "probe", None)),
        check_vma=False,
    )
```

profile of v0, /device:TPU:15, one launch (start us, length us, event | category | flops | bytes accessed | tf_op | source)
XLA Modules:
  0.0 295.4 jit_solution(17719606224704406409)
XLA Ops:
  0.6 2.2 collective-permute-start.8
  2.9 4.1 %collective-permute-start.7 = (f32[32,4,512]{2,1,0:T(4,128)}, f32[32,4,512]{2,1,0:T(4,128)S(1)}, u32[]{:S(2)}, u32[]{:S(2)}) collective-permute-start(f32[32,4,512]{2,1,0:T(4,128)} %param.8), channel_id=1, source_target_pairs={{0,4},{4,8},{8,12},{12,16},{16,20},{20,24},{24,28},{28,32},{32,36}... | collective-permute-start | bytes 786440 | tf_op jit(solution)/shard_map/ppermute | solution.py:29
  7.0 4.0 %collective-permute-done.8 = f32[32,4,512]{2,1,0:T(4,128)S(1)} collective-permute-done((f32[32,4,512]{2,1,0:T(4,128)}, f32[32,4,512]{2,1,0:T(4,128)S(1)}, u32[]{:S(2)}, u32[]{:S(2)}) %collective-permute-start.8) | collective-permute-done | bytes 262176 | tf_op jit(solution)/shard_map/ppermute | solution.py:32
  11.0 6.6 %collective-permute-done.7 = f32[32,4,512]{2,1,0:T(4,128)S(1)} collective-permute-done((f32[32,4,512]{2,1,0:T(4,128)}, f32[32,4,512]{2,1,0:T(4,128)S(1)}, u32[]{:S(2)}, u32[]{:S(2)}) %collective-permute-start.7) | collective-permute-done | bytes 262176 | tf_op jit(solution)/shard_map/ppermute | solution.py:29
  18.4 3.6 %collective-permute-start.10 = (f32[4,12,512]{2,1,0:T(8,128)S(1)}, f32[4,12,512]{2,1,0:T(8,128)S(1)}, u32[]{:S(2)}, u32[]{:S(2)}) collective-permute-start(f32[4,12,512]{2,1,0:T(8,128)S(1)} %get-tuple-element.21), channel_id=1, source_target_pairs={{1,0},{2,1},{3,2},{5,4},{6,5},{7,6},{9,8},{10,9},{11,10},{13,12},{... | collective-permute-start | bytes 294920 | tf_op jit(solution)/shard_map/ppermute | solution.py:32
  22.0 3.8 %collective-permute-start.9 = (f32[4,12,512]{2,1,0:T(8,128)S(1)}, f32[4,12,512]{2,1,0:T(8,128)S(1)}, u32[]{:S(2)}, u32[]{:S(2)}) collective-permute-start(f32[4,12,512]{2,1,0:T(8,128)S(1)} %get-tuple-element.20), channel_id=1, source_target_pairs={{0,1},{1,2},{2,3},{4,5},{5,6},{6,7},{8,9},{9,10},{10,11},{12,13},{... | collective-permute-start | bytes 294920 | tf_op jit(solution)/shard_map/ppermute | solution.py:29
  27.9 8.7 %collective-permute-start.3 = (f32[32,4,512]{2,1,0:T(4,128)}, f32[32,4,512]{2,1,0:T(4,128)S(1)}, u32[]{:S(2)}, u32[]{:S(2)}) collective-permute-start(f32[32,4,512]{2,1,0:T(4,128)} %get-tuple-element.17), channel_id=1, source_target_pairs={{0,32},{4,36},{8,40},{12,44},{16,48},{20,52},{24,56},{28,60},{32,6... | collective-permute-start | bytes 786440 | tf_op jit(solution)/shard_map/ppermute | solution.py:40
  38.8 4.4 %collective-permute-start = (f32[32,4,512]{2,1,0:T(4,128)S(1)}, f32[32,4,512]{2,1,0:T(4,128)}, u32[]{:S(2)}, u32[]{:S(2)}) collective-permute-start(f32[32,4,512]{2,1,0:T(4,128)S(1)} %copy-done.9), channel_id=1, source_target_pairs={{0,4},{4,0},{8,12},{12,8},{16,20},{20,16},{24,28},{28,24},{32,36},... | collective-permute-start | bytes 786440 | tf_op jit(solution)/shard_map/ppermute | solution.py:21
  44.1 5.2 %bitcast_add_fusion.1 = (f32[32,4,512]{2,1,0:T(4,128)S(1)}, f32[32,4,512]{2,1,0:T(4,128)}) fusion(f32[2,32,4,512]{3,2,1,0:T(4,128)S(1)} %copy-done.12, f32[32,4,512]{2,1,0:T(4,128)S(1)} %copy-done.9, f32[32,4,512]{2,1,0:T(4,128)S(1)} %copy-done.14, f32[32,4,512]{2,1,0:T(4,128)S(1)} %copy-done.8, f32[40,12,520]{2,1,0:T(8,128)S(1)} %select_maximum_fusion.12, ...), kind=kLoop, calls=%fused_computation.261 | loop fusion | flops 4718592 | bytes 4390912 | tf_op jit(solution)/shard_map/add | solution.py:83
  50.9 3.3 %collective-permute-start.19 = (f32[32,4,512]{2,1,0:T(4,128)S(1)}, f32[32,4,512]{2,1,0:T(4,128)S(1)}, u32[]{:S(2)}, u32[]{:S(2)}) collective-permute-start(f32[32,4,512]{2,1,0:T(4,128)S(1)} %get-tuple-element.4), channel_id=1, source_target_pairs={{4,0},{8,4},{12,8},{16,12},{20,16},{24,20},{28,24},{32,28},{36,32}... | collective-permute-start | bytes 786440 | tf_op jit(solution)/shard_map/ppermute | solution.py:32
  54.3 2.8 collective-permute-start.18
  64.0 5.7 %collective-permute-done.18 = f32[32,4,512]{2,1,0:T(4,128)S(1)} collective-permute-done((f32[32,4,512]{2,1,0:T(4,128)S(1)}, f32[32,4,512]{2,1,0:T(4,128)S(1)}, u32[]{:S(2)}, u32[]{:S(2)}) %collective-permute-start.18) | collective-permute-done | bytes 262176 | tf_op jit(solution)/shard_map/ppermute | solution.py:29
  69.8 2.4 collective-permute-start.21
  72.2 4.7 %collective-permute-start.20 = (f32[4,12,512]{2,1,0:T(8,128)S(1)}, f32[4,12,512]{2,1,0:T(8,128)S(1)}, u32[]{:S(2)}, u32[]{:S(2)}) collective-permute-start(f32[4,12,512]{2,1,0:T(8,128)S(1)} %get-tuple-element.18), channel_id=1, source_target_pairs={{0,1},{1,2},{2,3},{4,5},{5,6},{6,7},{8,9},{9,10},{10,11},{12,13},{... | collective-permute-start | bytes 294920 | tf_op jit(solution)/shard_map/ppermute | solution.py:29
  80.7 5.4 %collective-permute-done.12 = f32[32,8,512]{2,1,0:T(8,128)S(1)} collective-permute-done((f32[32,8,512]{2,1,0:T(8,128)S(1)}, f32[32,8,512]{2,1,0:T(8,128)S(1)}, u32[]{:S(2)}, u32[]{:S(2)}) %collective-permute-start.12) | collective-permute-done | bytes 524320 | tf_op jit(solution)/shard_map/ppermute | solution.py:21
  86.2 6.5 %collective-permute-start.13 = (f32[32,16,512]{2,1,0:T(8,128)S(1)}, f32[32,16,512]{2,1,0:T(8,128)S(1)}, u32[]{:S(2)}, u32[]{:S(2)}) collective-permute-start(f32[32,16,512]{2,1,0:T(8,128)S(1)} %maximum_select_fusion.4), channel_id=1, source_target_pairs={{0,16},{16,0},{4,20},{20,4},{8,24},{24,8},{12,28},{28,12},{32,48},... | collective-permute-start | bytes 3145736 | tf_op jit(solution)/shard_map/ppermute | solution.py:21
  92.7 5.2 %bitcast_add_fusion = (f32[32,4,512]{2,1,0:T(4,128)}, f32[32,4,512]{2,1,0:T(4,128)S(1)}) fusion(f32[2,32,4,512]{3,2,1,0:T(4,128)S(1)} %copy-done.13, f32[32,4,512]{2,1,0:T(4,128)S(1)} %copy-done.9, f32[32,4,512]{2,1,0:T(4,128)S(1)} %copy-done.8, f32[32,4,512]{2,1,0:T(4,128)S(1)} %get-tuple-element.4, f32[40,12,520]{2,1,0:T(8,128)S(1)} %select_maximum_fusion.8, ...), kind=kLoop, calls=%fused_computation.260 | loop fusion | flops 4718592 | bytes 4390912 | tf_op jit(solution)/shard_map/add | solution.py:83
  97.9 4.0 %select_maximum_fusion.4 = f32[40,40,520]{2,1,0:T(8,128)S(1)} fusion(f32[4,40,512]{2,1,0:T(8,128)S(1)} %collective-permute-done.6, f32[4,40,512]{2,1,0:T(8,128)S(1)} %collective-permute-done.5, f32[32,4,512]{2,1,0:T(4,128)S(1)} %collective-permute-done.4, f32[32,32,512]{2,1,0:T(8,128)S(1)} %copy-done, f32[32,4,512]{2,1,0:T(4,128)S(1)} %collective-permute-done.3), kind=kLoop, calls=%fused_computation.15 | loop fusion | flops 9984000 | bytes 6604800 | tf_op jit(solution)/shard_map/concatenate | solution.py:33
  102.0 3.3 %maximum_maximum_fusion = (f32[36,40,512]{2,1,0:T(8,128)S(1)}, f32[36,40,512]{2,1,0:T(8,128)}) fusion(f32[32,4,512]{2,1,0:T(4,128)} %copy-done.7, f32[32,32,512]{2,1,0:T(8,128)S(1)} %copy-done, f32[32,4,512]{2,1,0:T(4,128)} %copy-done.3, f32[4,40,512]{2,1,0:T(8,128)S(1)} %collective-permute-done.5, f32[4,40,512]{2,1,0:T(8,128)S(1)} %collective-permute-done.6), kind=kLoop, calls=%fused_computation.20 | loop fusion | flops 4423680 | bytes 9175040 | tf_op jit(solution)/shard_map/concatenate | solution.py:33
  109.3 41.6 %collective-permute-done.2 = f32[32,16,512]{2,1,0:T(8,128)S(1)} collective-permute-done((f32[32,16,512]{2,1,0:T(8,128)S(1)}, f32[32,16,512]{2,1,0:T(8,128)S(1)}, u32[]{:S(2)}, u32[]{:S(2)}) %collective-permute-start.2) | collective-permute-done | bytes 1048608 | tf_op jit(solution)/shard_map/ppermute | solution.py:21
  151.0 22.5 %collective-permute-done.13 = f32[32,16,512]{2,1,0:T(8,128)S(1)} collective-permute-done((f32[32,16,512]{2,1,0:T(8,128)S(1)}, f32[32,16,512]{2,1,0:T(8,128)S(1)}, u32[]{:S(2)}, u32[]{:S(2)}) %collective-permute-start.13) | collective-permute-done | bytes 1048608 | tf_op jit(solution)/shard_map/ppermute | solution.py:21
  174.4 19.9 %fusion.35 = f32[32,32,512]{2,1,0:T(8,128)S(1)} fusion(f32[32,32,512]{2,1,0:T(8,128)S(1)} %copy-done, f32[32,4,512]{2,1,0:T(4,128)} %copy-done.3, f32[40,40,520]{2,1,0:T(8,128)S(1)} %select_maximum_fusion.4, f32[32,36,512]{2,1,0:T(8,128)} %constant_dynamic-update-slice_fusion, f32[36,40,512]{2,1,0:T(8,128)} %get-tuple-element.11, ...), kind=kLoop, calls=%fused_computation.69 | loop fusion | flops 28835840 | bytes 54788096 | tf_op jit(solution)/shard_map/add | solution.py:95
  194.4 4.6 %collective-permute-start.15 = (f32[32,4,512]{2,1,0:T(4,128)S(1)}, f32[32,4,512]{2,1,0:T(4,128)S(1)}, u32[]{:S(2)}, u32[]{:S(2)}) collective-permute-start(f32[32,4,512]{2,1,0:T(4,128)S(1)} %get-tuple-element.15), channel_id=1, source_target_pairs={{32,0},{36,4},{40,8},{44,12},{48,16},{52,20},{56,24},{60,28},{64,3... | collective-permute-start | bytes 786440 | tf_op jit(solution)/shard_map/ppermute | solution.py:40
  199.0 4.6 %collective-permute-start.14 = (f32[32,4,512]{2,1,0:T(4,128)S(1)}, f32[32,4,512]{2,1,0:T(4,128)S(1)}, u32[]{:S(2)}, u32[]{:S(2)}) collective-permute-start(f32[32,4,512]{2,1,0:T(4,128)S(1)} %get-tuple-element.14), channel_id=1, source_target_pairs={{0,32},{4,36},{8,40},{12,44},{16,48},{20,52},{24,56},{28,60},{32,6... | collective-permute-start | bytes 786440 | tf_op jit(solution)/shard_map/ppermute | solution.py:40
  203.7 12.5 %collective-permute-done.15 = f32[32,4,512]{2,1,0:T(4,128)S(1)} collective-permute-done((f32[32,4,512]{2,1,0:T(4,128)S(1)}, f32[32,4,512]{2,1,0:T(4,128)S(1)}, u32[]{:S(2)}, u32[]{:S(2)}) %collective-permute-start.15) | collective-permute-done | bytes 262176 | tf_op jit(solution)/shard_map/ppermute | solution.py:40
  216.2 9.1 %collective-permute-done.14 = f32[32,4,512]{2,1,0:T(4,128)S(1)} collective-permute-done((f32[32,4,512]{2,1,0:T(4,128)S(1)}, f32[32,4,512]{2,1,0:T(4,128)S(1)}, u32[]{:S(2)}, u32[]{:S(2)}) %collective-permute-start.14) | collective-permute-done | bytes 262176 | tf_op jit(solution)/shard_map/ppermute | solution.py:40
  225.4 2.4 collective-permute-start.17
  227.8 4.7 %collective-permute-start.16 = (f32[4,40,512]{2,1,0:T(8,128)S(1)}, f32[4,40,512]{2,1,0:T(8,128)S(1)}, u32[]{:S(2)}, u32[]{:S(2)}) collective-permute-start(f32[4,40,512]{2,1,0:T(8,128)S(1)} %get-tuple-element.8), channel_id=1, source_target_pairs={{0,1},{1,2},{2,3},{4,5},{5,6},{6,7},{8,9},{9,10},{10,11},{12,13},{... | collective-permute-start | bytes 983048 | tf_op jit(solution)/shard_map/ppermute | solution.py:29
  236.5 2.2 maximum_maximum_fusion.1
  238.7 4.0 %select_maximum_fusion = f32[40,40,520]{2,1,0:T(8,128)S(1)} fusion(f32[4,40,512]{2,1,0:T(8,128)S(1)} %collective-permute-done.17, f32[4,40,512]{2,1,0:T(8,128)S(1)} %collective-permute-done.16, f32[32,4,512]{2,1,0:T(4,128)S(1)} %collective-permute-done.15, f32[32,32,512]{2,1,0:T(8,128)S(1)} %fusion.35, f32[32,4,512]{2,1,0:T(4,128)S(1)} %collective-permute-done.14), kind=kLoop, calls=%fused_computation.11 | loop fusion | flops 9984000 | bytes 6604800 | tf_op jit(solution)/shard_map/concatenate | solution.py:33
  242.7 37.2 %collective-permute-done.24 = f32[32,16,512]{2,1,0:T(8,128)S(1)} collective-permute-done((f32[32,16,512]{2,1,0:T(8,128)S(1)}, f32[32,16,512]{2,1,0:T(8,128)S(1)}, u32[]{:S(2)}, u32[]{:S(2)}) %collective-permute-start.24) | collective-permute-done | bytes 1048608 | tf_op jit(solution)/shard_map/ppermute | solution.py:21
  280.8 14.6 %fusion.12 = f32[32,32,512]{2,1,0:T(8,128)} fusion(f32[32,32,512]{2,1,0:T(8,128)S(1)} %fusion.35, f32[32,4,512]{2,1,0:T(4,128)S(1)} %collective-permute-done.15, f32[32,4,512]{2,1,0:T(4,128)S(1)} %collective-permute-done.14, f32[40,40,520]{2,1,0:T(8,128)S(1)} %select_maximum_fusion, f32[36,40,512]{2,1,0:T(8,128)} %get-tuple-element.7, ...), kind=kLoop, calls=%fused_computation.46 | loop fusion | flops 30932992 | bytes 46661632 | tf_op jit(solution)/shard_map/add | solution.py:95
  (72 shorter events, 28.6 us)
Async XLA Ops:
  0.6 42.6 %copy-start.8 = (f32[32,4,512]{2,1,0:T(4,128)S(1)}, f32[32,4,512]{2,1,0:T(4,128)}, u32[]{:S(2)}) copy-start(f32[32,4,512]{2,1,0:T(4,128)} %param.8) | copy-start | bytes 786436
  0.6 38.2 %copy-start.9 = (f32[32,4,512]{2,1,0:T(4,128)S(1)}, f32[32,4,512]{2,1,0:T(4,128)}, u32[]{:S(2)}) copy-start(f32[32,4,512]{2,1,0:T(4,128)} %param.10) | copy-start | bytes 786436
  0.6 10.3 %collective-permute-start.8 = (f32[32,4,512]{2,1,0:T(4,128)}, f32[32,4,512]{2,1,0:T(4,128)S(1)}, u32[]{:S(2)}, u32[]{:S(2)}) collective-permute-start(f32[32,4,512]{2,1,0:T(4,128)} %param.8), channel_id=1, source_target_pairs={{4,0},{8,4},{12,8},{16,12},{20,16},{24,20},{28,24},{32,28},{36,32}... | collective-permute-start | bytes 786440 | tf_op jit(solution)/shard_map/ppermute | solution.py:32
  2.9 14.7 %collective-permute-start.7 = (f32[32,4,512]{2,1,0:T(4,128)}, f32[32,4,512]{2,1,0:T(4,128)S(1)}, u32[]{:S(2)}, u32[]{:S(2)}) collective-permute-start(f32[32,4,512]{2,1,0:T(4,128)} %param.8), channel_id=1, source_target_pairs={{0,4},{4,8},{8,12},{12,16},{16,20},{20,24},{24,28},{28,32},{32,36}... | collective-permute-start | bytes 786440 | tf_op jit(solution)/shard_map/ppermute | solution.py:29
  18.4 25.7 %copy-start.12 = (f32[2,32,4,512]{3,2,1,0:T(4,128)S(1)}, f32[2,32,4,512]{3,2,1,0:T(4,128)}, u32[]{:S(2)}) copy-start(f32[2,32,4,512]{3,2,1,0:T(4,128)} %param.9) | copy-start | bytes 1572868
  18.4 25.7 %copy-start.14 = (f32[32,4,512]{2,1,0:T(4,128)S(1)}, f32[32,4,512]{2,1,0:T(4,128)}, u32[]{:S(2)}) copy-start(f32[32,4,512]{2,1,0:T(4,128)} %param.7) | copy-start | bytes 786436
  18.4 24.8 %collective-permute-start.10 = (f32[4,12,512]{2,1,0:T(8,128)S(1)}, f32[4,12,512]{2,1,0:T(8,128)S(1)}, u32[]{:S(2)}, u32[]{:S(2)}) collective-permute-start(f32[4,12,512]{2,1,0:T(8,128)S(1)} %get-tuple-element.21), channel_id=1, source_target_pairs={{1,0},{2,1},{3,2},{5,4},{6,5},{7,6},{9,8},{10,9},{11,10},{13,12},{... | collective-permute-start | bytes 294920 | tf_op jit(solution)/shard_map/ppermute | solution.py:32
  22.0 21.2 %collective-permute-start.9 = (f32[4,12,512]{2,1,0:T(8,128)S(1)}, f32[4,12,512]{2,1,0:T(8,128)S(1)}, u32[]{:S(2)}, u32[]{:S(2)}) collective-permute-start(f32[4,12,512]{2,1,0:T(8,128)S(1)} %get-tuple-element.20), channel_id=1, source_target_pairs={{0,1},{1,2},{2,3},{4,5},{5,6},{6,7},{8,9},{9,10},{10,11},{12,13},{... | collective-permute-start | bytes 294920 | tf_op jit(solution)/shard_map/ppermute | solution.py:29
  27.9 26.3 %collective-permute-start.3 = (f32[32,4,512]{2,1,0:T(4,128)}, f32[32,4,512]{2,1,0:T(4,128)S(1)}, u32[]{:S(2)}, u32[]{:S(2)}) collective-permute-start(f32[32,4,512]{2,1,0:T(4,128)} %get-tuple-element.17), channel_id=1, source_target_pairs={{0,32},{4,36},{8,40},{12,44},{16,48},{20,52},{24,56},{28,60},{32,6... | collective-permute-start | bytes 786440 | tf_op jit(solution)/shard_map/ppermute | solution.py:40
  36.6 20.5 %collective-permute-start.4 = (f32[32,4,512]{2,1,0:T(4,128)}, f32[32,4,512]{2,1,0:T(4,128)S(1)}, u32[]{:S(2)}, u32[]{:S(2)}) collective-permute-start(f32[32,4,512]{2,1,0:T(4,128)} %get-tuple-element.16), channel_id=1, source_target_pairs={{32,0},{36,4},{40,8},{44,12},{48,16},{52,20},{56,24},{60,28},{64,3... | collective-permute-start | bytes 786440 | tf_op jit(solution)/shard_map/ppermute | solution.py:40
  38.8 20.4 %collective-permute-start = (f32[32,4,512]{2,1,0:T(4,128)S(1)}, f32[32,4,512]{2,1,0:T(4,128)}, u32[]{:S(2)}, u32[]{:S(2)}) collective-permute-start(f32[32,4,512]{2,1,0:T(4,128)S(1)} %copy-done.9), channel_id=1, source_target_pairs={{0,4},{4,0},{8,12},{12,8},{16,20},{20,16},{24,28},{28,24},{32,36},... | collective-permute-start | bytes 786440 | tf_op jit(solution)/shard_map/ppermute | solution.py:21
  49.3 11.3 %collective-permute-start.11 = (f32[32,4,512]{2,1,0:T(4,128)}, f32[32,4,512]{2,1,0:T(4,128)}, u32[]{:S(2)}, u32[]{:S(2)}) collective-permute-start(f32[32,4,512]{2,1,0:T(4,128)} %get-tuple-element.5), channel_id=1, source_target_pairs={{0,4},{4,0},{8,12},{12,8},{16,20},{20,16},{24,28},{28,24},{32,36},... | collective-permute-start | bytes 786440 | tf_op jit(solution)/shard_map/ppermute | solution.py:21
  50.9 13.0 %collective-permute-start.19 = (f32[32,4,512]{2,1,0:T(4,128)S(1)}, f32[32,4,512]{2,1,0:T(4,128)S(1)}, u32[]{:S(2)}, u32[]{:S(2)}) collective-permute-start(f32[32,4,512]{2,1,0:T(4,128)S(1)} %get-tuple-element.4), channel_id=1, source_target_pairs={{4,0},{8,4},{12,8},{16,12},{20,16},{24,20},{28,24},{32,28},{36,32}... | collective-permute-start | bytes 786440 | tf_op jit(solution)/shard_map/ppermute | solution.py:32
  54.3 43.6 %copy-start.3 = (f32[32,4,512]{2,1,0:T(4,128)}, f32[32,4,512]{2,1,0:T(4,128)S(1)}, u32[]{:S(2)}) copy-start(f32[32,4,512]{2,1,0:T(4,128)S(1)} %collective-permute-done.3) | copy-start | bytes 786436
  54.3 15.4 %collective-permute-start.18 = (f32[32,4,512]{2,1,0:T(4,128)S(1)}, f32[32,4,512]{2,1,0:T(4,128)S(1)}, u32[]{:S(2)}, u32[]{:S(2)}) collective-permute-start(f32[32,4,512]{2,1,0:T(4,128)S(1)} %get-tuple-element.4), channel_id=1, source_target_pairs={{0,4},{4,8},{8,12},{12,16},{16,20},{20,24},{24,28},{28,32},{32,36}... | collective-permute-start | bytes 786440 | tf_op jit(solution)/shard_map/ppermute | solution.py:29
  57.1 40.8 %copy-start.7 = (f32[32,4,512]{2,1,0:T(4,128)}, f32[32,4,512]{2,1,0:T(4,128)S(1)}, u32[]{:S(2)}) copy-start(f32[32,4,512]{2,1,0:T(4,128)S(1)} %collective-permute-done.4) | copy-start | bytes 786436
  57.3 40.6 %collective-permute-start.6 = (f32[4,40,512]{2,1,0:T(8,128)S(1)}, f32[4,40,512]{2,1,0:T(8,128)S(1)}, u32[]{:S(2)}, u32[]{:S(2)}) collective-permute-start(f32[4,40,512]{2,1,0:T(8,128)S(1)} %get-tuple-element.13), channel_id=1, source_target_pairs={{1,0},{2,1},{3,2},{5,4},{6,5},{7,6},{9,8},{10,9},{11,10},{13,12},{... | collective-permute-start | bytes 983048 | tf_op jit(solution)/shard_map/ppermute | solution.py:32
  60.5 20.0 %collective-permute-start.1 = (f32[32,8,512]{2,1,0:T(8,128)S(1)}, f32[32,8,512]{2,1,0:T(8,128)S(1)}, u32[]{:S(2)}, u32[]{:S(2)}) collective-permute-start(f32[32,8,512]{2,1,0:T(8,128)S(1)} %maximum_select_fusion.6), channel_id=1, source_target_pairs={{0,8},{8,0},{4,12},{12,4},{16,24},{24,16},{20,28},{28,20},{32,40},... | collective-permute-start | bytes 1572872 | tf_op jit(solution)/shard_map/ppermute | solution.py:21
  62.1 24.0 %collective-permute-start.12 = (f32[32,8,512]{2,1,0:T(8,128)S(1)}, f32[32,8,512]{2,1,0:T(8,128)S(1)}, u32[]{:S(2)}, u32[]{:S(2)}) collective-permute-start(f32[32,8,512]{2,1,0:T(8,128)S(1)} %maximum_select_fusion.7), channel_id=1, source_target_pairs={{0,8},{8,0},{4,12},{12,4},{16,24},{24,16},{20,28},{28,20},{32,40},... | collective-permute-start | bytes 1572872 | tf_op jit(solution)/shard_map/ppermute | solution.py:21
  69.8 7.9 %collective-permute-start.21 = (f32[4,12,512]{2,1,0:T(8,128)S(1)}, f32[4,12,512]{2,1,0:T(8,128)S(1)}, u32[]{:S(2)}, u32[]{:S(2)}) collective-permute-start(f32[4,12,512]{2,1,0:T(8,128)S(1)} %get-tuple-element.19), channel_id=1, source_target_pairs={{1,0},{2,1},{3,2},{5,4},{6,5},{7,6},{9,8},{10,9},{11,10},{13,12},{... | collective-permute-start | bytes 294920 | tf_op jit(solution)/shard_map/ppermute | solution.py:32
  72.2 7.4 %collective-permute-start.20 = (f32[4,12,512]{2,1,0:T(8,128)S(1)}, f32[4,12,512]{2,1,0:T(8,128)S(1)}, u32[]{:S(2)}, u32[]{:S(2)}) collective-permute-start(f32[4,12,512]{2,1,0:T(8,128)S(1)} %get-tuple-element.18), channel_id=1, source_target_pairs={{0,1},{1,2},{2,3},{4,5},{5,6},{6,7},{8,9},{9,10},{10,11},{12,13},{... | collective-permute-start | bytes 294920 | tf_op jit(solution)/shard_map/ppermute | solution.py:29
  77.6 20.3 %collective-permute-start.5 = (f32[4,40,512]{2,1,0:T(8,128)S(1)}, f32[4,40,512]{2,1,0:T(8,128)S(1)}, u32[]{:S(2)}, u32[]{:S(2)}) collective-permute-start(f32[4,40,512]{2,1,0:T(8,128)S(1)} %get-tuple-element.12), channel_id=1, source_target_pairs={{0,1},{1,2},{2,3},{4,5},{5,6},{6,7},{8,9},{9,10},{10,11},{12,13},{... | collective-permute-start | bytes 983048 | tf_op jit(solution)/shard_map/ppermute | solution.py:29
  80.6 70.4 %collective-permute-start.2 = (f32[32,16,512]{2,1,0:T(8,128)S(1)}, f32[32,16,512]{2,1,0:T(8,128)S(1)}, u32[]{:S(2)}, u32[]{:S(2)}) collective-permute-start(f32[32,16,512]{2,1,0:T(8,128)S(1)} %maximum_select_fusion.3), channel_id=1, source_target_pairs={{0,16},{16,0},{4,20},{20,4},{8,24},{24,8},{12,28},{28,12},{32,48},... | collective-permute-start | bytes 3145736 | tf_op jit(solution)/shard_map/ppermute | solution.py:21
  86.2 87.3 %collective-permute-start.13 = (f32[32,16,512]{2,1,0:T(8,128)S(1)}, f32[32,16,512]{2,1,0:T(8,128)S(1)}, u32[]{:S(2)}, u32[]{:S(2)}) collective-permute-start(f32[32,16,512]{2,1,0:T(8,128)S(1)} %maximum_select_fusion.4), channel_id=1, source_target_pairs={{0,16},{16,0},{4,20},{20,4},{8,24},{24,8},{12,28},{28,12},{32,48},... | collective-permute-start | bytes 3145736 | tf_op jit(solution)/shard_map/ppermute | solution.py:21
  97.9 8.3 %collective-permute-start.22 = (f32[32,4,512]{2,1,0:T(4,128)S(1)}, f32[32,4,512]{2,1,0:T(4,128)S(1)}, u32[]{:S(2)}, u32[]{:S(2)}) collective-permute-start(f32[32,4,512]{2,1,0:T(4,128)S(1)} %get-tuple-element.3), channel_id=1, source_target_pairs={{0,4},{4,0},{8,12},{12,8},{16,20},{20,16},{24,28},{28,24},{32,36},... | collective-permute-start | bytes 786440 | tf_op jit(solution)/shard_map/ppermute | solution.py:21
  107.1 125.3 %collective-permute-start.23 = (f32[32,8,512]{2,1,0:T(8,128)}, f32[32,8,512]{2,1,0:T(8,128)}, u32[]{:S(2)}, u32[]{:S(2)}) collective-permute-start(f32[32,8,512]{2,1,0:T(8,128)} %maximum_select_fusion.8), channel_id=1, source_target_pairs={{0,8},{8,0},{4,12},{12,4},{16,24},{24,16},{20,28},{28,20},{32,40},... | collective-permute-start | bytes 1572872 | tf_op jit(solution)/shard_map/ppermute | solution.py:21
  194.4 21.7 %collective-permute-start.15 = (f32[32,4,512]{2,1,0:T(4,128)S(1)}, f32[32,4,512]{2,1,0:T(4,128)S(1)}, u32[]{:S(2)}, u32[]{:S(2)}) collective-permute-start(f32[32,4,512]{2,1,0:T(4,128)S(1)} %get-tuple-element.15), channel_id=1, source_target_pairs={{32,0},{36,4},{40,8},{44,12},{48,16},{52,20},{56,24},{60,28},{64,3... | collective-permute-start | bytes 786440 | tf_op jit(solution)/shard_map/ppermute | solution.py:40
  199.0 26.3 %collective-permute-start.14 = (f32[32,4,512]{2,1,0:T(4,128)S(1)}, f32[32,4,512]{2,1,0:T(4,128)S(1)}, u32[]{:S(2)}, u32[]{:S(2)}) collective-permute-start(f32[32,4,512]{2,1,0:T(4,128)S(1)} %get-tuple-element.14), channel_id=1, source_target_pairs={{0,32},{4,36},{8,40},{12,44},{16,48},{20,52},{24,56},{28,60},{32,6... | collective-permute-start | bytes 786440 | tf_op jit(solution)/shard_map/ppermute | solution.py:40
  225.4 9.9 %collective-permute-start.17 = (f32[4,40,512]{2,1,0:T(8,128)S(1)}, f32[4,40,512]{2,1,0:T(8,128)S(1)}, u32[]{:S(2)}, u32[]{:S(2)}) collective-permute-start(f32[4,40,512]{2,1,0:T(8,128)S(1)} %get-tuple-element.9), channel_id=1, source_target_pairs={{1,0},{2,1},{3,2},{5,4},{6,5},{7,6},{9,8},{10,9},{11,10},{13,12},{... | collective-permute-start | bytes 983048 | tf_op jit(solution)/shard_map/ppermute | solution.py:32
  227.8 8.7 %collective-permute-start.16 = (f32[4,40,512]{2,1,0:T(8,128)S(1)}, f32[4,40,512]{2,1,0:T(8,128)S(1)}, u32[]{:S(2)}, u32[]{:S(2)}) collective-permute-start(f32[4,40,512]{2,1,0:T(8,128)S(1)} %get-tuple-element.8), channel_id=1, source_target_pairs={{0,1},{1,2},{2,3},{4,5},{5,6},{6,7},{8,9},{9,10},{10,11},{12,13},{... | collective-permute-start | bytes 983048 | tf_op jit(solution)/shard_map/ppermute | solution.py:29
  234.2 45.6 %collective-permute-start.24 = (f32[32,16,512]{2,1,0:T(8,128)S(1)}, f32[32,16,512]{2,1,0:T(8,128)S(1)}, u32[]{:S(2)}, u32[]{:S(2)}) collective-permute-start(f32[32,16,512]{2,1,0:T(8,128)S(1)} %maximum_select_fusion.5), channel_id=1, source_target_pairs={{0,16},{16,0},{4,20},{20,4},{8,24},{24,8},{12,28},{28,12},{32,48},... | collective-permute-start | bytes 3145736 | tf_op jit(solution)/shard_map/ppermute | solution.py:21
  238.7 42.1 %copy-start.2 = (f32[32,16,512]{2,1,0:T(8,128)S(1)}, f32[32,16,512]{2,1,0:T(8,128)}, u32[]{:S(2)}) copy-start(f32[32,16,512]{2,1,0:T(8,128)} %copy-done.1) | copy-start | bytes 3145732
  (8 other events, 75.5 us)
where the time goes:
time: 296 us; the launch traced here: 295 us
  waiting for transfers between devices  148 us (50%)
  starting transfers between devices  73.1 us (25%)
  other arithmetic  66.7 us (23%)
  local copies, waits for them, and re-layouts  6.62 us (2%)
    ppermute x9, waiting for transfers between devices, partner_2(): return lax.ppermute(block, axis, route)  108 us
    add x2, other arithmetic, local(): 2.0 * newer_field - older_field + block_stiff * probe_lap  34.5 us
    ppermute x6, starting transfers between devices, with_halo(): lax.ppermute(lax.slice_in_dim(block, block.shape[dim] - width, None, axis...  22 us
    ppermute x4, waiting for transfers between devices, passed_along(): lax.ppermute(value, axis, [(source, source + steps) for source in range(f...  21.6 us
    ppermute x4, starting transfers between devices, passed_along(): lax.ppermute(value, axis, [(source, source + steps) for source in range(f...  20.1 us
    ppermute x6, starting transfers between devices, with_halo(): lax.ppermute(lax.slice_in_dim(block, 0, width, axis=dim), axis, backward)  15.8 us
    ppermute x9, starting transfers between devices, partner_2(): return lax.ppermute(block, axis, route)  15.2 us
    concatenate x6, other arithmetic, with_halo(): block = jnp.concatenate([low, block, high], axis=dim)  15.1 us
  transfers between devices with their start and end apart: 25, of which 13 were waited for; matrix products, arithmetic and copies ran while one was open for 19% of the time, Pallas kernels for 0%

commit v1 on v0

v1 whole, which is shorter than its diff:
```python
import functools

import jax
import jax.numpy as jnp
from jax import lax
from jax.experimental import pallas as pl
from jax.experimental.pallas import tpu as pltpu
from jax.sharding import PartitionSpec as P

coefficients = (-205.0 / 72.0, 8.0 / 5.0, -1.0 / 5.0, 8.0 / 315.0, -1.0 / 560.0)
SCALE = 5040
BAND = (0.0, 8064.0, -1008.0, 128.0, -9.0)

GROUP = 8
REACH = 4
MESH = pl.DeviceIdType.MESH
F32 = jnp.float32


def kernel(
    depth, rows, nx, n_probe, n_slab,
    iprev, inow, forcing, stiff, pprev, pnow, pert,
    probe_out, inc_out,
    U0, U1, UH, IP, FO, YE, XS, G, E0, E1, PP, PT, L, SB, DH, CL, B,
    ssG, rsG, ssU, rsU, ssD, rsD, ls,
):
    Pi = lax.axis_index("probe")
    Si = lax.axis_index("slab")
    p = Pi % GROUP
    zl = p // 2
    yl = p % 2
    z1 = zl + 1 - 2 * (zl % 2)
    z2 = (zl + 2) % 4
    z3 = 3 - zl
    base = Pi - p
    inner = jnp.logical_or(zl == 1, zl == 2)
    partner = Pi + 1 - 2 * yl
    own = rows // GROUP

    def zdev(k):
        return (base + (z1, z2, z3)[k] * 2 + yl, Si)

    def zslot(k):
        return (z1, z2, z3)[k] * 2 + yl

    has_p_lo, has_p_hi = Pi > 0, Pi < n_probe - 1
    has_b_lo, has_b_hi = Pi >= GROUP, Pi < n_probe - GROUP
    has_s_lo, has_s_hi = Si > 0, Si < n_slab - 1

    loads = [
        pltpu.make_async_copy(inow, U0.at[pl.ds(REACH, depth)], ls.at[0]),
        pltpu.make_async_copy(stiff, G.at[0, p], ls.at[1]),
        pltpu.make_async_copy(pnow, E0.at[pl.ds(REACH, depth), pl.ds(8, rows)], ls.at[2]),
        pltpu.make_async_copy(iprev, IP, ls.at[3]),
        pltpu.make_async_copy(forcing, FO, ls.at[4]),
        pltpu.make_async_copy(pprev, PP, ls.at[5]),
        pltpu.make_async_copy(pert, PT, ls.at[6]),
    ]
    for c in loads:
        c.start()

    bar = pltpu.get_barrier_semaphore()

    def hello(dev):
        pl.semaphore_signal(bar, inc=1, device_id=dev, device_id_type=MESH)

    for k in range(3):
        hello(zdev(k))
    hello((partner, Si))
    sides = [
        (has_p_lo, (Pi - 1, Si)), (has_p_hi, (Pi + 1, Si)),
        (has_b_lo, (Pi - GROUP, Si)), (has_b_hi, (Pi + GROUP, Si)),
        (has_s_lo, (Pi, Si - 1)), (has_s_hi, (Pi, Si + 1)),
    ]
    for cond, dev in sides:
        pl.when(cond)(functools.partial(hello, dev))
    peers = 4
    for cond, _ in sides:
        peers = peers + cond.astype(jnp.int32)
    pl.semaphore_wait(bar, peers)

    def remote(src, dst, ssem, rsem, dev):
        return pltpu.make_async_remote_copy(
            src_ref=src, dst_ref=dst, send_sem=ssem, recv_sem=rsem,
            device_id=dev, device_id_type=MESH,
        )

    pending = []

    def send(cond, desc):
        if cond is None:
            desc.start()
        else:
            pl.when(cond)(desc.start)
        pending.append((cond, desc))

    def rims_incident(step, src, U):
        send(has_p_lo, remote(src, UH.at[step, 1], ssU.at[step, 0], rsU.at[step, 1], (Pi - 1, Si)))
        send(has_p_hi, remote(src, UH.at[step, 0], ssU.at[step, 1], rsU.at[step, 0], (Pi + 1, Si)))
        send(has_s_lo, remote(src.at[pl.ds(0, REACH)], U.at[pl.ds(depth + REACH, REACH)],
                              ssU.at[step, 2], rsU.at[step, 3], (Pi, Si - 1)))
        send(has_s_hi, remote(src.at[pl.ds(depth - REACH, REACH)], U.at[pl.ds(0, REACH)],
                              ssU.at[step, 3], rsU.at[step, 2], (Pi, Si + 1)))

    def wait_incident(step, U):
        for side, cond in ((0, has_p_lo), (1, has_p_hi)):
            d = remote(UH.at[step, side], UH.at[step, side], ssU.at[step, side], rsU.at[step, side], (partner, Si))
            pl.when(cond)(d.wait_recv)
        for side, cond, at in ((2, has_s_lo, 0), (3, has_s_hi, depth + REACH)):
            r = U.at[pl.ds(at, REACH)]
            d = remote(r, r, ssU.at[step, side], rsU.at[step, side], (partner, Si))
            pl.when(cond)(d.wait_recv)

    def send_depth(step, low, high, E):
        send(has_s_lo, remote(low, E.at[pl.ds(depth + REACH, REACH), pl.ds(8, rows)],
                              ssD.at[step, 2], rsD.at[step, 3], (Pi, Si - 1)))
        send(has_s_hi, remote(high, E.at[pl.ds(0, REACH), pl.ds(8, rows)],
                              ssD.at[step, 3], rsD.at[step, 2], (Pi, Si + 1)))

    def wait_depth(step, E):
        for side, cond, at in ((2, has_s_lo, 0), (3, has_s_hi, depth + REACH)):
            r = E.at[pl.ds(at, REACH), pl.ds(8, rows)]
            d = remote(r, r, ssD.at[step, side], rsD.at[step, side], (partner, Si))
            pl.when(cond)(d.wait_recv)

    def send_rim(step, side):
        if side == 0:
            send(has_b_lo, remote(SB.at[step, 0], DH.at[step, 1], ssD.at[step, 0], rsD.at[step, 1], (Pi - GROUP, Si)))
        else:
            send(has_b_hi, remote(SB.at[step, 1], DH.at[step, 0], ssD.at[step, 1], rsD.at[step, 0], (Pi + GROUP, Si)))

    def wait_rim(step, side):
        r = DH.at[step, side]
        d = remote(r, r, ssD.at[step, side], rsD.at[step, side], (partner, Si))
        pl.when((has_b_lo, has_b_hi)[side])(d.wait_recv)

    def gather_own(a, src):
        dst = G.at[a, p]
        send(None, remote(src, dst, ssG.at[a, 1], rsG.at[a, p], zdev(0)))
        send(None, remote(src, dst, ssG.at[a, 2], rsG.at[a, p], zdev(1)))
        send(inner, remote(src, dst, ssG.at[a, 3], rsG.at[a, p], zdev(2)))
        send(None, remote(src, dst, ssG.at[a, 0], rsG.at[a, p], (partner, Si)))

    def gather_forward(a):
        for k in range(3):
            slot = zslot(k)
            r = G.at[a, slot]
            remote(r, r, ssG.at[a, 4 + k], rsG.at[a, slot], (partner, Si)).wait_recv()
            if k == 1:
                send(inner, remote(r, r, ssG.at[a, 7], rsG.at[a, slot], zdev(0)))
            send(None, remote(r, r, ssG.at[a, 4 + k], rsG.at[a, slot], (partner, Si)))

    def gather_wait(a, q):
        r = G.at[a, q]
        d = remote(r, r, ssG.at[a, 0], rsG.at[a, q], (partner, Si))
        pl.when((q % 2) != yl)(d.wait_recv)

    rims_incident(0, inow, U0)
    gather_own(0, stiff)
    send_depth(0, pnow.at[pl.ds(0, REACH)], pnow.at[pl.ds(depth - REACH, REACH)], E0)

    loads[2].wait()

    def pack(z, _):
        SB[0, 0, z] = E0[z + REACH, 8:12, :]
        SB[0, 1, z] = E0[z + REACH, rows + 4:rows + 8, :]
        return 0

    lax.fori_loop(0, depth, pack, 0)
    send_rim(0, 0)
    send_rim(0, 1)

    def band(i, _):
        r = lax.broadcasted_iota(jnp.int32, (64, nx), 0) + i * 64
        c = lax.broadcasted_iota(jnp.int32, (64, nx), 1)
        gap = jnp.abs(r - c)
        v = jnp.zeros((64, nx), F32)
        for j in range(1, 5):
            v = jnp.where(gap == j, BAND[j], v)
        B[pl.ds(pl.multiple_of(i * 64, 64), 64), :] = v.astype(jnp.bfloat16)
        return 0

    lax.fori_loop(0, nx // 64, band, 0)

    edge = jnp.zeros((8, nx), F32)

    def clear(z, _):
        for E in (E0, E1):
            E[z + REACH, 0:8, :] = edge
            E[z + REACH, rows + 8:rows + 16, :] = edge
        CL[z, 0, :, :] = edge
        CL[z, 1, :, :] = edge
        return 0

    lax.fori_loop(0, depth, clear, 0)
    for cond, at in ((has_s_lo, 0), (has_s_hi, depth + REACH)):

        @pl.when(jnp.logical_not(cond))
        def _(at=at):
            for i in range(REACH):
                for E in (E0, E1):
                    E[at + i, 8:8 + rows, :] = jnp.zeros((rows, nx), F32)
                for U in (U0, U1):
                    U[at + i] = jnp.zeros((own, nx), F32)

    for side, cp, cb in ((0, has_p_lo, has_b_lo), (1, has_p_hi, has_b_hi)):
        for R, cond in ((UH, cp), (DH, cb)):

            @pl.when(jnp.logical_not(cond))
            def _(R=R, side=side):
                def zero(z, _):
                    for step in range(2):
                        R[step, side, z] = jnp.zeros((own, nx), F32)
                    return 0

                lax.fori_loop(0, depth, zero, 0)

    def along_x(D):
        hi = D.astype(jnp.bfloat16)
        lo = (D - hi.astype(F32)).astype(jnp.bfloat16)
        X = jnp.dot(hi, B[...], preferred_element_type=F32)
        X = X + jnp.dot(lo, B[...], preferred_element_type=F32)
        return X * (1.0 / SCALE)

    def incident(step, U, older, into):
        def build(z, _):
            YE[z, 4:8, :] = UH[step, 0, z]
            YE[z, 8:12, :] = U[z + REACH]
            YE[z, 12:16, :] = UH[step, 1, z]
            return 0

        lax.fori_loop(0, depth, build, 0)
        XS[...] = along_x(YE[:, 8:16, :].reshape(depth * 8, nx)).reshape(depth, 8, nx)

        def point(z, _):
            c = U[z + REACH]
            acc = XS[z, 0:4, :] + (3.0 * coefficients[0]) * c
            for j in range(1, 5):
                acc = acc + coefficients[j] * (U[z + REACH - j] + U[z + REACH + j])
            for j in range(1, 5):
                acc = acc + coefficients[j] * (YE[z, 8 - j:12 - j, :] + YE[z, 8 + j:12 + j, :])
            G[1 + step, p, z] = acc
            into(z, 2.0 * c - older(z) + G[0, p, z] * acc + FO[step, z])
            return 0

        lax.fori_loop(0, depth, point, 0)

    def laplace(E):
        def wide(c, _):
            z0 = c * 8
            D = E[pl.ds(z0 + REACH, 8), 8:8 + rows, :].reshape(8 * rows, nx)
            L[pl.ds(z0, 8)] = along_x(D).reshape(8, rows, nx)
            return 0

        lax.fori_loop(0, depth // 8, wide, 0)

        def point(z, _):
            acc = L[z] + (3.0 * coefficients[0]) * E[z + REACH, 8:8 + rows, :]
            for j in range(1, 5):
                acc = acc + coefficients[j] * (E[z + REACH - j, 8:8 + rows, :] + E[z + REACH + j, 8:8 + rows, :])
            for j in range(1, 5):
                acc = acc + coefficients[j] * (
                    E[z + REACH, 8 - j:8 - j + rows, :] + E[z + REACH, 8 + j:8 + j + rows, :]
                )
            L[z] = acc
            return 0

        lax.fori_loop(0, depth, point, 0)

    def update(step, q, newer, older, into):
        gather_wait(0, q) if step == 0 else None
        gather_wait(1 + step, q)
        side = 0 if q == 0 else 1 if q == GROUP - 1 else None
        if side is not None:
            wait_rim(step, side)
        at = q * own

        def point(z, _):
            lap = L[z, at:at + own, :]
            if side == 0:
                CL[z, 0, 0:4, :] = DH[step, 0, z]
                for j in range(1, 5):
                    lap = lap + coefficients[j] * CL[z, 0, 4 - j:8 - j, :]
            if side == 1:
                CL[z, 1, 4:8, :] = DH[step, 1, z]
                for j in range(1, 5):
                    lap = lap + coefficients[j] * CL[z, 1, j:j + 4, :]
            value = (
                2.0 * newer(z, at) - older(z, at)
                + G[0, q, z] * (lap + 2.0 * PT[z, at:at + own, :] * G[1 + step, q, z])
            )
            into(z, at, value)
            if step == 0 and side is not None:
                SB[1, side, z] = value
            return 0

        lax.fori_loop(0, depth, point, 0)

    for i in (0, 1, 3, 4):
        loads[i].wait()
    wait_incident(0, U0)

    def into_u1(z, v):
        U1[z + REACH] = v

    incident(0, U0, lambda z: IP[z], into_u1)
    rims_incident(1, U1.at[pl.ds(REACH, depth)], U1)
    gather_own(1, G.at[1, p])

    gather_forward(0)
    wait_depth(0, E0)
    laplace(E0)

    wait_incident(1, U1)

    def into_out(z, v):
        inc_out[z] = v

    incident(1, U1, lambda z: U0[z + REACH], into_out)
    gather_own(2, G.at[2, p])
    gather_forward(1)

    loads[5].wait()
    loads[6].wait()

    def into_e1(z, at, v):
        E1[z + REACH, 8 + at:8 + at + own, :] = v

    def from_e(E):
        return lambda z, at: E[z + REACH, 8 + at:8 + at + own, :]

    for q in (0, GROUP - 1) + tuple(range(1, GROUP - 1)):
        update(0, q, from_e(E0), lambda z, at: PP[z, at:at + own, :], into_e1)
        if q == 0:
            send_rim(1, 0)
        if q == GROUP - 1:
            send_rim(1, 1)
    send_depth(1, E1.at[pl.ds(REACH, REACH), pl.ds(8, rows)], E1.at[pl.ds(depth, REACH), pl.ds(8, rows)], E1)

    gather_forward(2)
    wait_depth(1, E1)
    laplace(E1)

    def into_probe(z, at, v):
        probe_out[z, at:at + own, :] = v

    for q in tuple(range(1, GROUP - 1)) + (0, GROUP - 1):
        update(1, q, from_e(E1), from_e(E0), into_probe)

    for cond, d in pending:
        if cond is None:
            d.wait_send()
        else:
            pl.when(cond)(d.wait_send)


def local(n_probe, n_slab, iprev, inow, forcing, stiff, pprev, pnow, pert):
    depth, own, nx = inow.shape
    rows = pnow.shape[1]
    dma = pltpu.SemaphoreType.DMA
    vm = pltpu.VMEM
    return pl.pallas_call(
        functools.partial(kernel, depth, rows, nx, n_probe, n_slab),
        out_shape=(
            jax.ShapeDtypeStruct(pnow.shape, F32),
            jax.ShapeDtypeStruct(inow.shape, F32),
        ),
        in_specs=[pl.BlockSpec(memory_space=pl.ANY)] * 7,
        out_specs=(pl.BlockSpec(memory_space=pltpu.VMEM), pl.BlockSpec(memory_space=pltpu.VMEM)),
        scratch_shapes=[
            vm((depth + 8, own, nx), F32),
            vm((depth + 8, own, nx), F32),
            vm((2, 2, depth, own, nx), F32),
            vm((depth, own, nx), F32),
            vm((2, depth, own, nx), F32),
            vm((depth, 16, nx), F32),
            vm((depth, 8, nx), F32),
            vm((3, GROUP, depth, own, nx), F32),
            vm((depth + 8, rows + 16, nx), F32),
            vm((depth + 8, rows + 16, nx), F32),
            vm((depth, rows, nx), F32),
            vm((depth, rows, nx), F32),
            vm((depth, rows, nx), F32),
            vm((2, 2, depth, own, nx), F32),
            vm((2, 2, depth, own, nx), F32),
            vm((depth, 2, 8, nx), F32),
            vm((nx, nx), jnp.bfloat16),
            dma((3, 8)), dma((3, 8)), dma((2, 4)), dma((2, 4)), dma((2, 4)), dma((2, 4)), dma((7,)),
        ],
        compiler_params=pltpu.CompilerParams(
            collective_id=0, has_side_effects=True, vmem_limit_bytes=56 * 1024 * 1024
        ),
        name="born",
    )(iprev, inow, forcing, stiff, pprev, pnow, pert)


def solution(mesh):
    spec = P("slab", "probe", None)
    return jax.shard_map(
        functools.partial(local, mesh.shape["probe"], mesh.shape["slab"]),
        mesh=mesh,
        in_specs=(spec, spec, P(None, "slab", "probe", None), spec, spec, spec, spec),
        out_specs=(spec, spec),
        check_vma=False,
    )
```

time: 296 us -> 132 us (0.45)
  the two profiles are of different devices: /device:TPU:15 before, /device:TPU:26 now
where the time goes in v1:
time: 132 us; the launch traced here: 131 us
  Pallas kernels  127 us (96%)
  local copies, waits for them, and re-layouts  3.93 us (3%)
    pallas_call x1, Pallas kernels, local(): pl.pallas_call(functools.partial(kernel, depth, rows, nx, n_probe, n_slab...  127 us
    unnamed x4, local copies, waits for them, and re-layouts  3.93 us

profile of v1, /device:TPU:26, one launch (start us, length us, event | category | flops | bytes accessed | tf_op | source)
XLA Modules:
  0.0 131.1 jit_solution(9224961537592177845)
XLA Ops:
  0.6 126.5 %born.1 = (f32[32,32,512]{2,1,0:T(8,128)}, f32[32,4,512]{2,1,0:T(4,128)}) custom-call(f32[32,4,512]{2,1,0:T(4,128)} %iprev.1, f32[32,4,512]{2,1,0:T(4,128)} %inow.1, f32[2,32,4,512]{3,2,1,0:T(4,128)} %forcing.1, f32[32,4,512]{2,1,0:T(4,128)} %stiff.1, f32[32,32,512]{2,1,0:T(8,128)} %pprev.1, f32[32,32,512]{2,1,0:T(8,128)} %pnow.1, f32[32,32,512]{2,1,0:T(8,128)} %pert.1), custom_call_target="tpu_custom_call" | custom-call | tf_op jit(solution)/shard_map/born/pallas_call | solution.py:362
  127.2 0.0 copy-start
  127.2 3.2 %copy.11 = f32[32,32,512]{2,1,0:T(8,128)} copy(f32[32,32,512]{2,1,0:T(8,128)} %get-tuple-element.4) | data formatting | bytes 4194304
  130.4 0.0 copy-done
  130.4 0.7 copy.12
Async XLA Ops:
  127.2 3.2 %copy-start = (f32[32,4,512]{2,1,0:T(4,128)S(1)}, f32[32,4,512]{2,1,0:T(4,128)}, u32[]{:S(2)}) copy-start(f32[32,4,512]{2,1,0:T(4,128)} %get-tuple-element.5) | copy-start | bytes 786436

commit v2 on v1

v2 whole, which is shorter than its diff:
```python
import functools

import jax
import jax.numpy as jnp
from jax import lax
from jax.experimental import pallas as pl
from jax.experimental.pallas import tpu as pltpu
from jax.sharding import PartitionSpec as P

coefficients = (-205.0 / 72.0, 8.0 / 5.0, -1.0 / 5.0, 8.0 / 315.0, -1.0 / 560.0)
SCALE = 5040
BAND = (0.0, 8064.0, -1008.0, 128.0, -9.0)

GROUP = 8
REACH = 4
MESH = pl.DeviceIdType.MESH
RELAYED = (False, False)
ORDER = (
    "rims_u0", "own_s", "depth_0", "pack", "constants", "incident_0", "rims_u1", "own_0", "fwd_s0", "fwd_s1", "rims_0", "fwd_s2", "pass_0", "hear_0", "lap_00", "lap_01", "incident_1", "own_1", "fwd_00", "fwd_01", "fwd_02", "loads", "new_00", "new_07", "new_01", "new_02", "new_03", "new_04", "new_05", "new_06", "depth_1", "fwd_10", "fwd_11", "rims_1", "hear_1", "lap_10", "lap_11", "fwd_12", "pass_1", "new_11", "new_12", "new_13", "new_14", "new_15", "new_16", "new_10", "new_17",
)
F32 = jnp.float32


def kernel(
    depth, rows, nx, n_probe, n_slab,
    iprev, inow, forcing, stiff, pprev, pnow, pert,
    probe_out, inc_out,
    U0, U1, UH, IP, FO, YE, XS, G, E0, E1, PP, PT, L, SB, DH, RX, CL, B,
    ssG, rsG, ssU, rsU, ssD, rsD, ls,
):
    Pi = lax.axis_index("probe")
    Si = lax.axis_index("slab")
    p = Pi % GROUP
    zl = p // 2
    yl = p % 2
    z1 = zl + 1 - 2 * (zl % 2)
    z2 = (zl + 2) % 4
    z3 = 3 - zl
    base = Pi - p
    inner = jnp.logical_or(zl == 1, zl == 2)
    partner = Pi + 1 - 2 * yl
    own = rows // GROUP

    def zdev(k):
        return (base + (z1, z2, z3)[k] * 2 + yl, Si)

    def zslot(k):
        return (z1, z2, z3)[k] * 2 + yl

    has_p_lo, has_p_hi = Pi > 0, Pi < n_probe - 1
    has_b_lo, has_b_hi = Pi >= GROUP, Pi < n_probe - GROUP
    has_s_lo, has_s_hi = Si > 0, Si < n_slab - 1
    block, last = Pi // GROUP, n_probe // GROUP - 1
    from_lo, relay_lo, to_lo = block == 2, block == 0, block == 1
    from_hi, relay_hi, to_hi = block == last - 2, block == last, block == last - 1

    loads = [
        pltpu.make_async_copy(inow, U0.at[pl.ds(REACH, depth)], ls.at[0]),
        pltpu.make_async_copy(stiff, G.at[0, p], ls.at[1]),
        pltpu.make_async_copy(pnow, E0.at[pl.ds(REACH, depth), pl.ds(8, rows)], ls.at[2]),
        pltpu.make_async_copy(iprev, IP, ls.at[3]),
        pltpu.make_async_copy(forcing, FO, ls.at[4]),
        pltpu.make_async_copy(pprev, PP, ls.at[5]),
        pltpu.make_async_copy(pert, PT, ls.at[6]),
    ]
    for c in loads:
        c.start()

    bar = pltpu.get_barrier_semaphore()

    def hello(dev):
        pl.semaphore_signal(bar, inc=1, device_id=dev, device_id_type=MESH)

    for k in range(3):
        hello(zdev(k))
    hello((partner, Si))
    sides = [
        (has_p_lo, (Pi - 1, Si)), (has_p_hi, (Pi + 1, Si)),
        (has_b_lo, (Pi - GROUP, Si)), (has_b_hi, (Pi + GROUP, Si)),
        (has_s_lo, (Pi, Si - 1)), (has_s_hi, (Pi, Si + 1)),
        (Pi > 1, (Pi - 2, Si)), (Pi < n_probe - 2, (Pi + 2, Si)),
        (jnp.logical_or(from_lo, relay_hi), (Pi - 2 * GROUP, Si)),
        (jnp.logical_or(from_hi, relay_lo), (Pi + 2 * GROUP, Si)),
    ]
    for cond, dev in sides:
        pl.when(cond)(functools.partial(hello, dev))
    peers = 4
    for cond, _ in sides:
        peers = peers + cond.astype(jnp.int32)
    pl.semaphore_wait(bar, peers)

    def remote(src, dst, ssem, rsem, dev):
        return pltpu.make_async_remote_copy(
            src_ref=src, dst_ref=dst, send_sem=ssem, recv_sem=rsem,
            device_id=dev, device_id_type=MESH,
        )

    pending = []

    def send(cond, desc):
        if cond is None:
            desc.start()
        else:
            pl.when(cond)(desc.start)
        pending.append((cond, desc))

    half = depth // 2
    near, far = pl.ds(0, half), pl.ds(half, half)
    lower, upper = yl == 0, yl == 1

    def rims_incident(step, src, U):
        def to(cond, dev, side, part, k):
            send(cond, remote(src.at[part], UH.at[step, side, part], ssU.at[step, k], rsU.at[step, side, k % 2], dev))

        for part, k in ((near, 0), (far, 1)):
            to(lower, (partner, Si), 0, part, k)
            to(upper, (partner, Si), 1, part, k)
        send(has_s_lo, remote(src.at[pl.ds(0, REACH)], U.at[pl.ds(depth + REACH, REACH)],
                              ssU.at[step, 4], rsU.at[step, 3, 0], (Pi, Si - 1)))
        send(has_s_hi, remote(src.at[pl.ds(depth - REACH, REACH)], U.at[pl.ds(0, REACH)],
                              ssU.at[step, 5], rsU.at[step, 2, 0], (Pi, Si + 1)))
        for part, k in ((near, 2), (far, 3))[:1 if RELAYED[step] else 2]:
            to(jnp.logical_and(lower, has_p_lo), (Pi - 1, Si), 1, part, k)
            to(jnp.logical_and(upper, has_p_hi), (Pi + 1, Si), 0, part, k)

    def arrived(step, side, k):
        r = UH.at[step, side, (near, far)[k]]
        remote(r, r, ssU.at[step, 3], rsU.at[step, side, k], (partner, Si)).wait_recv()

    def pass_incident(step):
        for mine, there, side, dev in (
            (lower, Pi < n_probe - 2, 1, (Pi + 2, Si)),
            (upper, Pi > 1, 0, (Pi - 2, Si)),
        ):

            @pl.when(mine)
            def _(side=side):
                arrived(step, side, 1)

            send(jnp.logical_and(mine, there),
                 remote(UH.at[step, side, far], UH.at[step, 1 - side, far], ssU.at[step, 3],
                        rsU.at[step, 1 - side, 1], dev))

    def wait_incident(step, U):
        for mine, side, there in ((lower, 1, has_p_lo), (upper, 0, has_p_hi)):

            @pl.when(mine)
            def _(side=side):
                arrived(step, side, 0)
                if not RELAYED[step]:
                    arrived(step, side, 1)

            @pl.when(jnp.logical_and(mine, there))
            def _(side=side):
                arrived(step, 1 - side, 0)
                arrived(step, 1 - side, 1)

        for side, cond, at in ((2, has_s_lo, 0), (3, has_s_hi, depth + REACH)):
            r = U.at[pl.ds(at, REACH)]
            d = remote(r, r, ssU.at[step, 3], rsU.at[step, side, 0], (partner, Si))
            pl.when(cond)(d.wait_recv)

    def send_depth(step, low, high, E):
        send(has_s_lo, remote(low, E.at[pl.ds(depth + REACH, REACH), pl.ds(8, rows)],
                              ssD.at[step, 2, 0], rsD.at[step, 3, 0], (Pi, Si - 1)))
        send(has_s_hi, remote(high, E.at[pl.ds(0, REACH), pl.ds(8, rows)],
                              ssD.at[step, 3, 0], rsD.at[step, 2, 0], (Pi, Si + 1)))

    def wait_depth(step, E):
        for side, cond, at in ((2, has_s_lo, 0), (3, has_s_hi, depth + REACH)):
            r = E.at[pl.ds(at, REACH), pl.ds(8, rows)]
            d = remote(r, r, ssD.at[step, side, 0], rsD.at[step, side, 0], (partner, Si))
            pl.when(cond)(d.wait_recv)

    def send_rim(step, side):
        cond, by_x, shift, hop = (
            (has_b_lo, from_lo, -GROUP, -2 * GROUP), (has_b_hi, from_hi, GROUP, 2 * GROUP)
        )[side]

        def to(cond, dst, part, k, rsem, dev):
            send(cond, remote(SB.at[step, side, part], dst, ssD.at[step, side, k], rsem, dev))

        out = DH.at[step, 1 - side]
        to(cond, out.at[near], near, 0, rsD.at[step, 1 - side, 0], (Pi + shift, Si))
        to(jnp.logical_and(cond, jnp.logical_not(by_x)), out.at[far], far, 1,
           rsD.at[step, 1 - side, 1], (Pi + shift, Si))
        to(by_x, RX.at[step], far, 2, rsD.at[step, 2, 1], (Pi + hop, Si))

    def pass_rim(step):
        for cond, side, shift in ((relay_lo, 1, GROUP), (relay_hi, 0, -GROUP)):

            @pl.when(cond)
            def _():
                remote(RX.at[step], RX.at[step], ssD.at[step, 3, 1], rsD.at[step, 2, 1], (partner, Si)).wait_recv()

            send(cond, remote(RX.at[step], DH.at[step, side, far], ssD.at[step, 2, 1], rsD.at[step, side, 1],
                              (Pi + shift, Si)))

    def wait_rim(step, side):
        for part, k in ((near, 0), (far, 1)):
            r = DH.at[step, side, part]
            d = remote(r, r, ssD.at[step, side, k], rsD.at[step, side, k], (partner, Si))
            pl.when((has_b_lo, has_b_hi)[side])(d.wait_recv)

    def gather_own(a, src):
        dst = G.at[a, p]
        send(None, remote(src, dst, ssG.at[a, 1], rsG.at[a, p], zdev(0)))
        send(None, remote(src, dst, ssG.at[a, 2], rsG.at[a, p], zdev(1)))
        send(inner, remote(src, dst, ssG.at[a, 3], rsG.at[a, p], zdev(2)))
        send(None, remote(src, dst, ssG.at[a, 0], rsG.at[a, p], (partner, Si)))

    def forward(a, k):
        slot = zslot(k)
        r = G.at[a, slot]
        remote(r, r, ssG.at[a, 4 + k], rsG.at[a, slot], (partner, Si)).wait_recv()
        if k == 1:
            send(inner, remote(r, r, ssG.at[a, 7], rsG.at[a, slot], zdev(0)))
        send(None, remote(r, r, ssG.at[a, 4 + k], rsG.at[a, slot], (partner, Si)))

    def gather_wait(a, q):
        r = G.at[a, q]
        d = remote(r, r, ssG.at[a, 0], rsG.at[a, q], (partner, Si))
        pl.when((q % 2) != yl)(d.wait_recv)

    def pack():
        loads[2].wait()

        def row(z, _):
            SB[0, 0, z] = E0[z + REACH, 8:12, :]
            SB[0, 1, z] = E0[z + REACH, rows + 4:rows + 8, :]
            return 0

        lax.fori_loop(0, depth, row, 0)

    def constants():
        def band(i, _):
            r = lax.broadcasted_iota(jnp.int32, (64, nx), 0) + i * 64
            c = lax.broadcasted_iota(jnp.int32, (64, nx), 1)
            gap = jnp.abs(r - c)
            v = jnp.zeros((64, nx), F32)
            for j in range(1, 5):
                v = jnp.where(gap == j, BAND[j], v)
            B[pl.ds(pl.multiple_of(i * 64, 64), 64), :] = v.astype(jnp.bfloat16)
            return 0

        lax.fori_loop(0, nx // 64, band, 0)

        edge = jnp.zeros((8, nx), F32)

        def clear(z, _):
            for E in (E0, E1):
                E[z + REACH, 0:8, :] = edge
                E[z + REACH, rows + 8:rows + 16, :] = edge
            CL[z, 0, :, :] = edge
            CL[z, 1, :, :] = edge
            return 0

        lax.fori_loop(0, depth, clear, 0)
        for cond, at in ((has_s_lo, 0), (has_s_hi, depth + REACH)):

            @pl.when(jnp.logical_not(cond))
            def _(at=at):
                for i in range(REACH):
                    for E in (E0, E1):
                        E[at + i, 8:8 + rows, :] = jnp.zeros((rows, nx), F32)
                    for U in (U0, U1):
                        U[at + i] = jnp.zeros((own, nx), F32)

        for side, cp, cb in ((0, has_p_lo, has_b_lo), (1, has_p_hi, has_b_hi)):
            for R, cond in ((UH, cp), (DH, cb)):

                @pl.when(jnp.logical_not(cond))
                def _(R=R, side=side):
                    def zero(z, _):
                        for step in range(2):
                            R[step, side, z] = jnp.zeros((own, nx), F32)
                        return 0

                    lax.fori_loop(0, depth, zero, 0)

    def along_x(D):
        hi = D.astype(jnp.bfloat16)
        lo = (D - hi.astype(F32)).astype(jnp.bfloat16)
        X = jnp.dot(hi, B[...], preferred_element_type=F32)
        X = X + jnp.dot(lo, B[...], preferred_element_type=F32)
        return X * (1.0 / SCALE)

    def incident(step, U, older, into):
        def build(z, _):
            YE[z, 4:8, :] = UH[step, 0, z]
            YE[z, 8:12, :] = U[z + REACH]
            YE[z, 12:16, :] = UH[step, 1, z]
            return 0

        lax.fori_loop(0, depth, build, 0)
        XS[...] = along_x(YE[:, 8:16, :].reshape(depth * 8, nx)).reshape(depth, 8, nx)

        def point(z, _):
            c = U[z + REACH]
            acc = XS[z, 0:4, :] + (3.0 * coefficients[0]) * c
            for j in range(1, 5):
                acc = acc + coefficients[j] * (U[z + REACH - j] + U[z + REACH + j])
            for j in range(1, 5):
                acc = acc + coefficients[j] * (YE[z, 8 - j:12 - j, :] + YE[z, 8 + j:12 + j, :])
            G[1 + step, p, z] = acc
            into(z, 2.0 * c - older(z) + G[0, p, z] * acc + FO[step, z])
            return 0

        lax.fori_loop(0, depth, point, 0)

    def laplace(E, part, parts):
        first, end = part * depth // parts, (part + 1) * depth // parts

        def wide(c, _):
            z0 = c * 8
            D = E[pl.ds(z0 + REACH, 8), 8:8 + rows, :].reshape(8 * rows, nx)
            L[pl.ds(z0, 8)] = along_x(D).reshape(8, rows, nx)
            return 0

        lax.fori_loop(first // 8, end // 8, wide, 0)

        def point(z, _):
            acc = L[z] + (3.0 * coefficients[0]) * E[z + REACH, 8:8 + rows, :]
            for j in range(1, 5):
                acc = acc + coefficients[j] * (E[z + REACH - j, 8:8 + rows, :] + E[z + REACH + j, 8:8 + rows, :])
            for j in range(1, 5):
                acc = acc + coefficients[j] * (
                    E[z + REACH, 8 - j:8 - j + rows, :] + E[z + REACH, 8 + j:8 + j + rows, :]
                )
            L[z] = acc
            return 0

        lax.fori_loop(first, end, point, 0)

    def update(step, q, newer, older, into):
        gather_wait(0, q) if step == 0 else None
        gather_wait(1 + step, q)
        side = 0 if q == 0 else 1 if q == GROUP - 1 else None
        if side is not None:
            wait_rim(step, side)
        at = q * own

        def point(z, _):
            lap = L[z, at:at + own, :]
            if side == 0:
                CL[z, 0, 0:4, :] = DH[step, 0, z]
                for j in range(1, 5):
                    lap = lap + coefficients[j] * CL[z, 0, 4 - j:8 - j, :]
            if side == 1:
                CL[z, 1, 4:8, :] = DH[step, 1, z]
                for j in range(1, 5):
                    lap = lap + coefficients[j] * CL[z, 1, j:j + 4, :]
            value = (
                2.0 * newer(z, at) - older(z, at)
                + G[0, q, z] * (lap + 2.0 * PT[z, at:at + own, :] * G[1 + step, q, z])
            )
            into(z, at, value)
            if step == 0 and side is not None:
                SB[1, side, z] = value
            return 0

        lax.fori_loop(0, depth, point, 0, unroll=4)

    def into_u1(z, v):
        U1[z + REACH] = v

    def into_out(z, v):
        inc_out[z] = v

    def into_e1(z, at, v):
        E1[z + REACH, 8 + at:8 + at + own, :] = v

    def into_probe(z, at, v):
        probe_out[z, at:at + own, :] = v

    def from_e(E):
        return lambda z, at: E[z + REACH, 8 + at:8 + at + own, :]

    def incident_0():
        for i in (0, 1, 3, 4):
            loads[i].wait()
        wait_incident(0, U0)
        incident(0, U0, lambda z: IP[z], into_u1)

    def incident_1():
        wait_incident(1, U1)
        incident(1, U1, lambda z: U0[z + REACH], into_out)

    def update_0(q):
        update(0, q, from_e(E0), lambda z, at: PP[z, at:at + own, :], into_e1)

    def update_1(q):
        update(1, q, from_e(E1), from_e(E0), into_probe)

    low, high = pl.ds(REACH, REACH), pl.ds(depth, REACH)
    tasks = {
        "rims_u0": lambda: rims_incident(0, inow, U0),
        "rims_u1": lambda: rims_incident(1, U1.at[pl.ds(REACH, depth)], U1),
        "pass_u0": lambda: pass_incident(0),
        "pass_u1": lambda: pass_incident(1),
        "own_s": lambda: gather_own(0, stiff),
        "own_0": lambda: gather_own(1, G.at[1, p]),
        "own_1": lambda: gather_own(2, G.at[2, p]),
        "depth_0": lambda: send_depth(0, pnow.at[pl.ds(0, REACH)], pnow.at[pl.ds(depth - REACH, REACH)], E0),
        "depth_1": lambda: send_depth(1, E1.at[low, pl.ds(8, rows)], E1.at[high, pl.ds(8, rows)], E1),
        "pack": pack,
        "constants": constants,
        "rims_0": lambda: (send_rim(0, 0), send_rim(0, 1)),
        "rims_1": lambda: (send_rim(1, 0), send_rim(1, 1)),
        "pass_0": lambda: pass_rim(0),
        "pass_1": lambda: pass_rim(1),
        "incident_0": incident_0,
        "incident_1": incident_1,
        "hear_0": lambda: wait_depth(0, E0),
        "hear_1": lambda: wait_depth(1, E1),
        "loads": lambda: (loads[5].wait(), loads[6].wait()),
    }
    for k in range(3):
        for a, name in enumerate("s01"):
            tasks["fwd_%s%d" % (name, k)] = functools.partial(forward, a, k)
    for part in range(2):
        tasks["lap_0%d" % part] = functools.partial(laplace, E0, part, 2)
        tasks["lap_1%d" % part] = functools.partial(laplace, E1, part, 2)
    for q in range(GROUP):
        tasks["new_0%d" % q] = functools.partial(update_0, q)
        tasks["new_1%d" % q] = functools.partial(update_1, q)
    for name in ORDER:
        tasks[name]()

    for cond, d in pending:
        if cond is None:
            d.wait_send()
        else:
            pl.when(cond)(d.wait_send)


def local(n_probe, n_slab, iprev, inow, forcing, stiff, pprev, pnow, pert):
    depth, own, nx = inow.shape
    rows = pnow.shape[1]
    dma = pltpu.SemaphoreType.DMA
    vm = pltpu.VMEM
    return fresh(*pl.pallas_call(
        functools.partial(kernel, depth, rows, nx, n_probe, n_slab),
        out_shape=(pltpu.VMEM(pnow.shape, F32), pltpu.VMEM(inow.shape, F32)),
        in_specs=[pl.BlockSpec(memory_space=pltpu.HBM)] * 7,
        out_specs=(pl.BlockSpec(memory_space=pltpu.VMEM), pl.BlockSpec(memory_space=pltpu.VMEM)),
        scratch_shapes=[
            vm((depth + 8, own, nx), F32),
            vm((depth + 8, own, nx), F32),
            vm((2, 2, depth, own, nx), F32),
            vm((depth, own, nx), F32),
            vm((2, depth, own, nx), F32),
            vm((depth, 16, nx), F32),
            vm((depth, 8, nx), F32),
            vm((3, GROUP, depth, own, nx), F32),
            vm((depth + 8, rows + 16, nx), F32),
            vm((depth + 8, rows + 16, nx), F32),
            vm((depth, rows, nx), F32),
            vm((depth, rows, nx), F32),
            vm((depth, rows, nx), F32),
            vm((2, 2, depth, own, nx), F32),
            vm((2, 2, depth, own, nx), F32),
            vm((2, depth // 2, own, nx), F32),
            vm((depth, 2, 8, nx), F32),
            vm((nx, nx), jnp.bfloat16),
            dma((3, 8)), dma((3, 8)), dma((2, 6)), dma((2, 4, 2)), dma((2, 4, 3)), dma((2, 4, 2)), dma((7,)),
        ],
        compiler_params=pltpu.CompilerParams(
            collective_id=0, has_side_effects=True, vmem_limit_bytes=48 * 1024 * 1024
        ),
        name="born",
    )(*(pltpu.with_memory_space_constraint(v, pltpu.HBM) for v in (iprev, inow, forcing, stiff, pprev, pnow, pert))))


def hand_over(a, b, a_out, b_out, sems):
    moves = [pltpu.make_async_copy(a, a_out, sems.at[0]), pltpu.make_async_copy(b, b_out, sems.at[1])]
    for m in moves:
        m.start()
    for m in moves:
        m.wait()


def fresh(a, b):
    vmem, any_ = pl.BlockSpec(memory_space=pltpu.VMEM), pl.BlockSpec(memory_space=pl.ANY)
    return pl.pallas_call(
        hand_over,
        out_shape=(jax.ShapeDtypeStruct(a.shape, F32), jax.ShapeDtypeStruct(b.shape, F32)),
        in_specs=[vmem, vmem], out_specs=(any_, any_), name="fresh",
        scratch_shapes=[pltpu.SemaphoreType.DMA((2,))],
    )(pltpu.with_memory_space_constraint(a, pltpu.VMEM), pltpu.with_memory_space_constraint(b, pltpu.VMEM))


def solution(mesh):
    spec = P("slab", "probe", None)
    return jax.shard_map(
        functools.partial(local, mesh.shape["probe"], mesh.shape["slab"]),
        mesh=mesh,
        in_specs=(spec, spec, P(None, "slab", "probe", None), spec, spec, spec, spec),
        out_specs=(spec, spec),
        check_vma=False,
    )
```

time: 132 us -> 123 us (0.932)
  the two profiles are of different devices: /device:TPU:26 before, /device:TPU:13 now
where the time goes in v2:
time: 123 us
  Pallas kernels  122 us (99%)
    pallas_call x1, Pallas kernels, local(): pl.pallas_call(functools.partial(kernel, depth, rows, nx, n_probe, n_slab...  121 us

profile of v2, /device:TPU:13, one launch (start us, length us, event | category | flops | bytes accessed | tf_op | source)
XLA Modules:
  0.0 123.1 jit_solution(1590731615462464502)
XLA Ops:
  0.6 121.1 %born.1 = (f32[32,32,512]{2,1,0:T(8,128)S(1)}, f32[32,4,512]{2,1,0:T(4,128)S(1)}) custom-call(f32[32,4,512]{2,1,0:T(4,128)} %iprev.1, f32[32,4,512]{2,1,0:T(4,128)} %inow.1, f32[2,32,4,512]{3,2,1,0:T(4,128)} %forcing.1, f32[32,4,512]{2,1,0:T(4,128)} %stiff.1, f32[32,32,512]{2,1,0:T(8,128)} %pprev.1, f32[32,32,512]{2,1,0:T(8,128)} %pnow.1, f32[32,32,512]{2,1,0:T(8,128)} %pert.1), custom_call_target="tpu_custom_call" | custom-call | tf_op jit(solution)/shard_map/born/pallas_call | solution.py:442
  121.7 1.4 %fresh.1 = (f32[32,32,512]{2,1,0:T(8,128)}, f32[32,4,512]{2,1,0:T(4,128)}) custom-call(f32[32,32,512]{2,1,0:T(8,128)S(1)} %get-tuple-element.4.a, f32[32,4,512]{2,1,0:T(4,128)S(1)} %get-tuple-element.5.b), custom_call_target="tpu_custom_call" | custom-call | tf_op jit(solution)/shard_map/fresh/pallas_call | solution.py:485

commit v3 on v2

--- a/solution.py
+++ b/solution.py
@@ -14,9 +14,9 @@
 GROUP = 8
 REACH = 4
 MESH = pl.DeviceIdType.MESH
-RELAYED = (False, False)
+RELAYED = (True, False)
 ORDER = (
-    "rims_u0", "own_s", "depth_0", "pack", "constants", "incident_0", "rims_u1", "own_0", "fwd_s0", "fwd_s1", "rims_0", "fwd_s2", "pass_0", "hear_0", "lap_00", "lap_01", "incident_1", "own_1", "fwd_00", "fwd_01", "fwd_02", "loads", "new_00", "new_07", "new_01", "new_02", "new_03", "new_04", "new_05", "new_06", "depth_1", "fwd_10", "fwd_11", "rims_1", "hear_1", "lap_10", "lap_11", "fwd_12", "pass_1", "new_11", "new_12", "new_13", "new_14", "new_15", "new_16", "new_10", "new_17",
+    "rims_u0", "own_s_away", "depth_0", "pack", "constants", "pass_u0", "own_s_along", "incident_0", "rims_u1", "own_0", "fwd_s0", "fwd_s1", "fwd_s2", "hear_0", "lap_00", "lap_01", "fwd_00_inner", "fwd_01_inner", "rims_0", "pass_0", "incident_1", "own_1", "fwd_00_outer", "fwd_01_outer", "fwd_02", "loads", "new_00", "new_07", "new_01", "new_02", "new_03", "new_04", "new_05", "new_06", "depth_1", "fwd_10", "fwd_11", "rims_1", "hear_1", "lap_10", "lap_11", "fwd_12", "pass_1", "new_11", "new_12", "new_13", "new_14", "new_15", "new_16", "new_10", "new_17",
 )
 F32 = jnp.float32
 
@@ -119,7 +119,7 @@
                               ssU.at[step, 4], rsU.at[step, 3, 0], (Pi, Si - 1)))
         send(has_s_hi, remote(src.at[pl.ds(depth - REACH, REACH)], U.at[pl.ds(0, REACH)],
                               ssU.at[step, 5], rsU.at[step, 2, 0], (Pi, Si + 1)))
-        for part, k in ((near, 2), (far, 3))[:1 if RELAYED[step] else 2]:
+        for part, k in () if RELAYED[step] else ((near, 2), (far, 3)):
             to(jnp.logical_and(lower, has_p_lo), (Pi - 1, Si), 1, part, k)
             to(jnp.logical_and(upper, has_p_hi), (Pi + 1, Si), 0, part, k)
 
@@ -132,22 +132,19 @@
             (lower, Pi < n_probe - 2, 1, (Pi + 2, Si)),
             (upper, Pi > 1, 0, (Pi - 2, Si)),
         ):
+            for part, k in ((near, 0), (far, 1)):
+                pl.when(mine)(functools.partial(arrived, step, side, k))
+                send(jnp.logical_and(mine, there),
+                     remote(UH.at[step, side, part], UH.at[step, 1 - side, part], ssU.at[step, 2 + k],
+                            rsU.at[step, 1 - side, k], dev))
+
+    def wait_incident(step, U):
+        for mine, side, there in ((lower, 1, has_p_lo), (upper, 0, has_p_hi)):
 
             @pl.when(mine)
             def _(side=side):
-                arrived(step, side, 1)
-
-            send(jnp.logical_and(mine, there),
-                 remote(UH.at[step, side, far], UH.at[step, 1 - side, far], ssU.at[step, 3],
-                        rsU.at[step, 1 - side, 1], dev))
-
-    def wait_incident(step, U):
-        for mine, side, there in ((lower, 1, has_p_lo), (upper, 0, has_p_hi)):
-
-            @pl.when(mine)
-            def _(side=side):
-                arrived(step, side, 0)
                 if not RELAYED[step]:
+                    arrived(step, side, 0)
                     arrived(step, side, 1)
 
             @pl.when(jnp.logical_and(mine, there))
@@ -172,10 +169,12 @@
             d = remote(r, r, ssD.at[step, side, 0], rsD.at[step, side, 0], (partner, Si))
             pl.when(cond)(d.wait_recv)
 
-    def send_rim(step, side):
+    def send_rim(step, side, role=None):
         cond, by_x, shift, hop = (
             (has_b_lo, from_lo, -GROUP, -2 * GROUP), (has_b_hi, from_hi, GROUP, 2 * GROUP)
         )[side]
+        if role is not None:
+            cond, by_x = jnp.logical_and(cond, role), jnp.logical_and(by_x, role)
 
         def to(cond, dst, part, k, rsem, dev):
             send(cond, remote(SB.at[step, side, part], dst, ssD.at[step, side, k], rsem, dev))
@@ -202,20 +201,28 @@
             d = remote(r, r, ssD.at[step, side, k], rsD.at[step, side, k], (partner, Si))
             pl.when((has_b_lo, has_b_hi)[side])(d.wait_recv)
 
-    def gather_own(a, src):
+    def gather_own(a, src, part="all"):
         dst = G.at[a, p]
-        send(None, remote(src, dst, ssG.at[a, 1], rsG.at[a, p], zdev(0)))
-        send(None, remote(src, dst, ssG.at[a, 2], rsG.at[a, p], zdev(1)))
-        send(inner, remote(src, dst, ssG.at[a, 3], rsG.at[a, p], zdev(2)))
-        send(None, remote(src, dst, ssG.at[a, 0], rsG.at[a, p], (partner, Si)))
-
-    def forward(a, k):
+        for k, up, there in ((0, zl % 2 == 0, None), (1, zl < 2, None), (2, zl == 1, inner)):
+            if part != "all":
+                way = (up == upper) if part == "away" else (up != upper)
+                there = way if there is None else jnp.logical_and(there, way)
+            send(there, remote(src, dst, ssG.at[a, 1 + k], rsG.at[a, p], zdev(k)))
+        if part != "along":
+            send(None, remote(src, dst, ssG.at[a, 0], rsG.at[a, p], (partner, Si)))
+
+    def forward(a, k, role=None):
         slot = zslot(k)
         r = G.at[a, slot]
-        remote(r, r, ssG.at[a, 4 + k], rsG.at[a, slot], (partner, Si)).wait_recv()
+        arrival = remote(r, r, ssG.at[a, 4 + k], rsG.at[a, slot], (partner, Si))
+        if role is None:
+            arrival.wait_recv()
+        else:
+            pl.when(role)(arrival.wait_recv)
         if k == 1:
-            send(inner, remote(r, r, ssG.at[a, 7], rsG.at[a, slot], zdev(0)))
-        send(None, remote(r, r, ssG.at[a, 4 + k], rsG.at[a, slot], (partner, Si)))
+            relay = inner if role is None else jnp.logical_and(inner, role)
+            send(relay, remote(r, r, ssG.at[a, 7], rsG.at[a, slot], zdev(0)))
+        send(role, remote(r, r, ssG.at[a, 4 + k], rsG.at[a, slot], (partner, Si)))
 
     def gather_wait(a, q):
         r = G.at[a, q]
@@ -399,6 +406,10 @@
         "pass_u0": lambda: pass_incident(0),
         "pass_u1": lambda: pass_incident(1),
         "own_s": lambda: gather_own(0, stiff),
+        "own_s_away": lambda: gather_own(0, stiff, "away"),
+        "own_s_along": lambda: gather_own(0, stiff, "along"),
+        "own_0_away": lambda: gather_own(1, G.at[1, p], "away"),
+        "own_0_along": lambda: gather_own(1, G.at[1, p], "along"),
         "own_0": lambda: gather_own(1, G.at[1, p]),
         "own_1": lambda: gather_own(2, G.at[2, p]),
         "depth_0": lambda: send_depth(0, pnow.at[pl.ds(0, REACH)], pnow.at[pl.ds(depth - REACH, REACH)], E0),
@@ -415,9 +426,15 @@
         "hear_1": lambda: wait_depth(1, E1),
         "loads": lambda: (loads[5].wait(), loads[6].wait()),
     }
+    outer = jnp.logical_not(inner)
     for k in range(3):
         for a, name in enumerate("s01"):
             tasks["fwd_%s%d" % (name, k)] = functools.partial(forward, a, k)
+            tasks["fwd_%s%d_inner" % (name, k)] = functools.partial(forward, a, k, inner)
+            tasks["fwd_%s%d_outer" % (name, k)] = functools.partial(forward, a, k, outer)
+    for step in range(2):
+        tasks["rims_%d_inner" % step] = lambda step=step: (send_rim(step, 0, inner), send_rim(step, 1, inner))
+        tasks["rims_%d_outer" % step] = lambda step=step: (send_rim(step, 0, outer), send_rim(step, 1, outer))
     for part in range(2):
         tasks["lap_0%d" % part] = functools.partial(laplace, E0, part, 2)
         tasks["lap_1%d" % part] = functools.partial(laplace, E1, part, 2)

time: 123 us -> 122 us (level)
  the two profiles are of different devices: /device:TPU:13 before, /device:TPU:26 now
where the time goes in v3:
time: 122 us
  Pallas kernels  121 us (99%)
    pallas_call x1, Pallas kernels, local(): pl.pallas_call(functools.partial(kernel, depth, rows, nx, n_probe, n_slab...  120 us

profile of v3, /device:TPU:26, one launch (start us, length us, event | category | flops | bytes accessed | tf_op | source)
XLA Modules:
  0.0 122.0 jit_solution(10446592690015322551)
XLA Ops:
  0.6 119.9 %born.1 = (f32[32,32,512]{2,1,0:T(8,128)S(1)}, f32[32,4,512]{2,1,0:T(4,128)S(1)}) custom-call(f32[32,4,512]{2,1,0:T(4,128)} %iprev.1, f32[32,4,512]{2,1,0:T(4,128)} %inow.1, f32[2,32,4,512]{3,2,1,0:T(4,128)} %forcing.1, f32[32,4,512]{2,1,0:T(4,128)} %stiff.1, f32[32,32,512]{2,1,0:T(8,128)} %pprev.1, f32[32,32,512]{2,1,0:T(8,128)} %pnow.1, f32[32,32,512]{2,1,0:T(8,128)} %pert.1), custom_call_target="tpu_custom_call" | custom-call | tf_op jit(solution)/shard_map/born/pallas_call | solution.py:459
  120.6 1.4 %fresh.1 = (f32[32,32,512]{2,1,0:T(8,128)}, f32[32,4,512]{2,1,0:T(4,128)}) custom-call(f32[32,32,512]{2,1,0:T(8,128)S(1)} %get-tuple-element.4.a, f32[32,4,512]{2,1,0:T(4,128)S(1)} %get-tuple-element.5.b), custom_call_target="tpu_custom_call" | custom-call | tf_op jit(solution)/shard_map/fresh/pallas_call | solution.py:502

commit v4 on v3

--- a/solution.py
+++ b/solution.py
@@ -16,7 +16,7 @@
 MESH = pl.DeviceIdType.MESH
 RELAYED = (True, False)
 ORDER = (
-    "rims_u0", "own_s_away", "depth_0", "pack", "constants", "pass_u0", "own_s_along", "incident_0", "rims_u1", "own_0", "fwd_s0", "fwd_s1", "fwd_s2", "hear_0", "lap_00", "lap_01", "fwd_00_inner", "fwd_01_inner", "rims_0", "pass_0", "incident_1", "own_1", "fwd_00_outer", "fwd_01_outer", "fwd_02", "loads", "new_00", "new_07", "new_01", "new_02", "new_03", "new_04", "new_05", "new_06", "depth_1", "fwd_10", "fwd_11", "rims_1", "hear_1", "lap_10", "lap_11", "fwd_12", "pass_1", "new_11", "new_12", "new_13", "new_14", "new_15", "new_16", "new_10", "new_17",
+    "rims_u0", "own_s_away", "depth_0", "pack", "constants", "pass_u0", "own_s_along", "incident_0", "rims_u1", "own_0", "fwd_s0", "fwd_s1", "fwd_s2", "hear_0", "fwd_00_inner", "fwd_01_inner", "rims_0", "lap_00", "lap_01", "pass_0", "incident_1", "own_1", "fwd_00_outer", "fwd_01_outer", "fwd_02", "loads", "new_00", "new_07", "new_01", "new_02", "new_03", "new_04", "new_05", "new_06", "depth_1", "fwd_10", "fwd_11", "rims_1", "hear_1", "lap_10", "lap_11", "fwd_12", "pass_1", "new_11", "new_12", "new_13", "new_14", "new_15", "new_16", "new_10", "new_17",
 )
 F32 = jnp.float32
 

time: 122 us -> 121 us (level)
  no operation moved by 1% of the time
where the time goes in v4:
time: 121 us
  Pallas kernels  121 us (100%)
    pallas_call x1, Pallas kernels, local(): pl.pallas_call(functools.partial(kernel, depth, rows, nx, n_probe, n_slab...  119 us

profile of v4, /device:TPU:26, one launch (start us, length us, event | category | flops | bytes accessed | tf_op | source)
XLA Modules:
  0.0 121.3 jit_solution(1258867537725055843)
XLA Ops:
  0.6 119.2 %born.1 = (f32[32,32,512]{2,1,0:T(8,128)S(1)}, f32[32,4,512]{2,1,0:T(4,128)S(1)}) custom-call(f32[32,4,512]{2,1,0:T(4,128)} %iprev.1, f32[32,4,512]{2,1,0:T(4,128)} %inow.1, f32[2,32,4,512]{3,2,1,0:T(4,128)} %forcing.1, f32[32,4,512]{2,1,0:T(4,128)} %stiff.1, f32[32,32,512]{2,1,0:T(8,128)} %pprev.1, f32[32,32,512]{2,1,0:T(8,128)} %pnow.1, f32[32,32,512]{2,1,0:T(8,128)} %pert.1), custom_call_target="tpu_custom_call" | custom-call | tf_op jit(solution)/shard_map/born/pallas_call | solution.py:459
  119.9 1.4 %fresh.1 = (f32[32,32,512]{2,1,0:T(8,128)}, f32[32,4,512]{2,1,0:T(4,128)}) custom-call(f32[32,32,512]{2,1,0:T(8,128)S(1)} %get-tuple-element.4.a, f32[32,4,512]{2,1,0:T(4,128)S(1)} %get-tuple-element.5.b), custom_call_target="tpu_custom_call" | custom-call | tf_op jit(solution)/shard_map/fresh/pallas_call | solution.py:502

commit v5 on v4

--- a/solution.py
+++ b/solution.py
@@ -16,7 +16,7 @@
 MESH = pl.DeviceIdType.MESH
 RELAYED = (True, False)
 ORDER = (
-    "rims_u0", "own_s_away", "depth_0", "pack", "constants", "pass_u0", "own_s_along", "incident_0", "rims_u1", "own_0", "fwd_s0", "fwd_s1", "fwd_s2", "hear_0", "fwd_00_inner", "fwd_01_inner", "rims_0", "lap_00", "lap_01", "pass_0", "incident_1", "own_1", "fwd_00_outer", "fwd_01_outer", "fwd_02", "loads", "new_00", "new_07", "new_01", "new_02", "new_03", "new_04", "new_05", "new_06", "depth_1", "fwd_10", "fwd_11", "rims_1", "hear_1", "lap_10", "lap_11", "fwd_12", "pass_1", "new_11", "new_12", "new_13", "new_14", "new_15", "new_16", "new_10", "new_17",
+    "rims_u0", "own_s_away", "depth_0", "pack", "constants", "pass_u0", "own_s_along", "incident_0", "rims_u1", "own_0", "fwd_s0", "fwd_s1", "fwd_s2", "hear_0", "fwd_00_inner", "fwd_01_inner", "rims_0", "incident_1", "own_1", "lap_00", "lap_01", "pass_0", "fwd_00_outer", "fwd_01_outer", "fwd_02", "loads", "new_00", "new_07", "new_01", "new_02", "new_03", "new_04", "new_05", "new_06", "depth_1", "fwd_10", "fwd_11", "rims_1", "hear_1", "lap_10", "lap_11", "fwd_12", "pass_1", "new_11", "new_12", "new_13", "new_14", "new_15", "new_16", "new_10", "new_17",
 )
 F32 = jnp.float32
 

time: 121 us -> 121 us (level)
  no operation moved by 1% of the time
where the time goes in v5:
time: 121 us
  Pallas kernels  121 us (100%)
    pallas_call x1, Pallas kernels, local(): pl.pallas_call(functools.partial(kernel, depth, rows, nx, n_probe, n_slab...  119 us

profile of v5, /device:TPU:26, one launch (start us, length us, event | category | flops | bytes accessed | tf_op | source)
XLA Modules:
  0.0 121.3 jit_solution(7648667648181367022)
XLA Ops:
  0.6 119.2 %born.1 = (f32[32,32,512]{2,1,0:T(8,128)S(1)}, f32[32,4,512]{2,1,0:T(4,128)S(1)}) custom-call(f32[32,4,512]{2,1,0:T(4,128)} %iprev.1, f32[32,4,512]{2,1,0:T(4,128)} %inow.1, f32[2,32,4,512]{3,2,1,0:T(4,128)} %forcing.1, f32[32,4,512]{2,1,0:T(4,128)} %stiff.1, f32[32,32,512]{2,1,0:T(8,128)} %pprev.1, f32[32,32,512]{2,1,0:T(8,128)} %pnow.1, f32[32,32,512]{2,1,0:T(8,128)} %pert.1), custom_call_target="tpu_custom_call" | custom-call | tf_op jit(solution)/shard_map/born/pallas_call | solution.py:459
  119.9 1.4 %fresh.1 = (f32[32,32,512]{2,1,0:T(8,128)}, f32[32,4,512]{2,1,0:T(4,128)}) custom-call(f32[32,32,512]{2,1,0:T(8,128)S(1)} %get-tuple-element.4.a, f32[32,4,512]{2,1,0:T(4,128)S(1)} %get-tuple-element.5.b), custom_call_target="tpu_custom_call" | custom-call | tf_op jit(solution)/shard_map/fresh/pallas_call | solution.py:502
